TPU v7x, 256 devices: a whole 4x4x8 slice. The times are simulated.
256 devices in a mesh: gx: 8 (over x_hi, y), gy: 32 (over x_lo, z, core).
Axes of the slice: x: 4 (x_hi: 2, x_lo: 2; x = x_hi * 2 + x_lo), y: 4, z: 8, core: 2. Of those that a mesh axis runs over, the one named last changes fastest.
Arguments:
- features: bfloat16 [8, 32, 4, 512, 128], P('gx', 'gy')
- occupancy: int32 [8, 32, 4, 512], P('gx', 'gy'), may hold values 0 or 1
- counts: int32 [8, 32], P('gx', 'gy'), may hold values from 1 to 4, as said below
- kernel_map: int32 [8, 32, 4, 27], P('gx', 'gy'), may hold values from 0 to 16, as said below
- x_send: int32 [8, 32, 2, 2], P('gx', 'gy'), may hold values from 0 to 4, as said below
- y_send: int32 [8, 32, 2, 4], P('gx', 'gy'), may hold values from 0 to 8, as said below
- weight: bfloat16 [27, 128, 128], replicated, may hold values from -0.109375 to 0.109375
- norm_gain: float32 [128], replicated, may hold values from 0.5 to 1.5
- norm_shift: float32 [128], replicated, may hold values from -3 to 3
- cotangent: bfloat16 [8, 32, 4, 512, 128], P('gx', 'gy'), may hold values from -6 to 6
Outputs:
- activations: bfloat16 [8, 32, 4, 512, 128], P('gx', 'gy')
- features_grad: bfloat16 [8, 32, 4, 512, 128], P('gx', 'gy')
- weight_grad: float32 [27, 128, 128], replicated
- gain_grad: float32 [128], replicated
- shift_grad: float32 [128], replicated
Inputs may be any that keep to these rules, and one draw needn't show every extreme that they name: `counts`: slots at or past a tile's count are empty; some tile is full. `kernel_map`: rows are numbered as in the brick table; 16 stands for an empty neighbour, and so does every tap of an empty slot. `x_send`: listed slots are live and distinct, in increasing order, followed by 4 as padding. `y_send`: entries index the first 8 rows of the sender's brick table, distinct, followed by 4 + 2 * 2 as padding.
All inputs are finite; a program needn't handle non-finite values. No bound on the sum of `occupancy` on one device may be relied on, other than what follows from the above.
Results may differ from a plain program's by a relative error of at most 0.0049.
Values may be sent and summed in bfloat16 or wider, within the bound.
No kernel may reach another device: no remote copies, remote signals or barrier semaphores. Data moves between devices by JAX's collectives and lax.ppermute only.
A program may use at most 192 MiB of HBM per device.

v0:
```python
import functools

import jax
import jax.numpy as jnp
from jax import lax
from jax.experimental import pallas as pl
from jax.experimental.pallas import tpu as pltpu
from jax.sharding import PartitionSpec as P

EDGE = 8
PLANE = 64
VOX = 512
CH = 128
SLOTS = 4
HX = 2
HY = 4
EPSILON = 1e-05
F32 = jnp.float32
BF16 = jnp.bfloat16

VM = pl.BlockSpec(memory_space=pltpu.VMEM)
SM = pl.BlockSpec(memory_space=pltpu.SMEM)
MAIN = 224
EXTRA = 48
FACE_ROWS = HY * PLANE + 16
MIB = 1024 * 1024
CROSS = ("xh", "y", "xl")


def params(limit=20):
    return pltpu.CompilerParams(vmem_limit_bytes=limit * MIB)


def cost(flops, moved):
    return pl.CostEstimate(flops=flops, bytes_accessed=moved, transcendentals=0)


def shape(dims, kind):
    return jax.ShapeDtypeStruct(dims, kind)


def pick_x(sends_ref, own_ref, low_ref, high_ref, faces):
    for side, out_ref in ((0, low_ref), (1, high_ref)):
        start, stop = (0, VOX) if not faces else ((0, PLANE), (VOX - PLANE, VOX))[side]
        for k in range(HX):
            row = sends_ref[side, k]
            brick = own_ref[jnp.minimum(row, SLOTS - 1), start:stop, :]
            out_ref[k] = jnp.where(row < SLOTS, brick, jnp.zeros_like(brick))


def x_shapes(faces):
    send = shape((HX, PLANE if faces else VOX, CH), BF16)
    return (send, send)


def prepare_kernel(
    counts_ref, sends_ref, feat_ref, occ_ref, own_ref, mask_ref, low_ref, high_ref, *, faces
):
    for s in range(SLOTS):
        live = (s < counts_ref[0, 0]).astype(F32)
        for k in range(VOX // CH):
            row = occ_ref[s : s + 1, k * CH : (k + 1) * CH].astype(F32) * live
            column = jnp.transpose(jnp.broadcast_to(row, (CH, CH)))
            rows = pl.ds(k * CH, CH)
            mask_ref[s, rows, :] = column.astype(BF16)
            own_ref[s, rows, :] = (feat_ref[s, rows, :].astype(F32) * column).astype(BF16)
    pick_x(sends_ref, own_ref, low_ref, high_ref, faces)


def prepare(counts, sends_x, features, occupancy, faces):
    return pl.pallas_call(
        functools.partial(prepare_kernel, faces=faces),
        out_shape=(shape((SLOTS, VOX, CH), BF16),) * 2 + x_shapes(faces),
        in_specs=[SM, SM, VM, VM],
        out_specs=(VM, VM, VM, VM),
        compiler_params=params(),
        cost_estimate=cost(1 << 20, 2 << 20),
        name="prepare",
    )(counts, sends_x, features, occupancy)


def pick_y_kernel(sends_ref, own_ref, xl_ref, xu_ref, low_ref, high_ref):
    for side, out_ref in ((0, low_ref), (1, high_ref)):
        for k in range(HY):
            row = sends_ref[side, k]

            @pl.when(row < SLOTS)
            def _():
                out_ref[k] = own_ref[jnp.minimum(row, SLOTS - 1)]

            @pl.when((row >= SLOTS) & (row < SLOTS + HX))
            def _():
                out_ref[k] = xl_ref[jnp.clip(row - SLOTS, 0, HX - 1)]

            @pl.when((row >= SLOTS + HX) & (row < SLOTS + 2 * HX))
            def _():
                out_ref[k] = xu_ref[jnp.clip(row - SLOTS - HX, 0, HX - 1)]

            @pl.when(row >= SLOTS + 2 * HX)
            def _():
                out_ref[k] = jnp.zeros((VOX, CH), BF16)


def pick_y_faces_kernel(sends_ref, own_ref, xl_ref, xu_ref, low_ref, high_ref):
    lines = lax.broadcasted_iota(jnp.int32, (16, CH), 0)
    for side, out_ref in ((0, low_ref), (1, high_ref)):
        skip = 0 if side == 0 else PLANE - 16

        def edge(block):
            block = block.astype(F32)
            return block[:EDGE] if side == 0 else block[EDGE:]

        origin = jnp.zeros((16, CH), F32)
        for k in range(HY):
            row = sends_ref[side, k]
            rows = pl.ds(k * PLANE, PLANE)
            lower = (row >= SLOTS) & (row < SLOTS + HX)
            upper = (row >= SLOTS + HX) & (row < SLOTS + 2 * HX)
            code = jnp.where(lower, 1.0, jnp.where(upper, 2.0, 0.0))
            origin = jnp.where(lines == k, code, origin)

            @pl.when(row < SLOTS)
            def _():
                brick = jnp.minimum(row, SLOTS - 1)
                parts = [
                    edge(own_ref[brick, a * PLANE + skip : a * PLANE + skip + 16, :])
                    for a in range(EDGE)
                ]
                out_ref[rows, :] = jnp.concatenate(parts, axis=0).astype(BF16)

            @pl.when(lower)
            def _():
                part = edge(xl_ref[jnp.clip(row - SLOTS, 0, HX - 1), skip : skip + 16, :])
                empty = jnp.zeros((PLANE - EDGE, CH), F32)
                out_ref[rows, :] = jnp.concatenate((empty, part), axis=0).astype(BF16)

            @pl.when(upper)
            def _():
                part = edge(xu_ref[jnp.clip(row - SLOTS - HX, 0, HX - 1), skip : skip + 16, :])
                empty = jnp.zeros((PLANE - EDGE, CH), F32)
                out_ref[rows, :] = jnp.concatenate((part, empty), axis=0).astype(BF16)

            @pl.when(row >= SLOTS + 2 * HX)
            def _():
                out_ref[rows, :] = jnp.zeros((PLANE, CH), BF16)

        out_ref[HY * PLANE : FACE_ROWS, :] = origin.astype(BF16)


def pick_y(sends_y, own, xl, xu, faces):
    send = shape((FACE_ROWS, CH) if faces else (HY, VOX, CH), BF16)
    return pl.pallas_call(
        pick_y_faces_kernel if faces else pick_y_kernel,
        out_shape=(send, send),
        in_specs=[SM, VM, VM, VM],
        out_specs=(VM, VM),
        compiler_params=params(),
        cost_estimate=cost(1 << 20, 2 << 20),
        name="pick_y",
    )(sends_y, own, xl, xu)


def axis_size(axes):
    size = 1
    for axis in axes:
        size *= lax.axis_size(axis)
    return size


def neighbours(low, high, axis):
    size = axis_size(axis)
    up = [(i, i + 1) for i in range(size - 1)]
    down = [(j, i) for i, j in up]
    return lax.ppermute(high, axis, up), lax.ppermute(low, axis, down)


def fill_columns(map_ref, slot, table_ref, x9_ref):
    sub = lax.broadcasted_iota(jnp.int32, (EDGE + 2, EDGE, CH), 1)
    for a in range(-1, EDGE + 1):
        move = -1 if a < 0 else (1 if a >= EDGE else 0)
        base = (a % EDGE) * PLANE
        spans = []
        for r in (-1, 0, 1):
            tap = 9 * (move + 1) + r + 1
            before = table_ref[map_ref[slot, tap], base + 48 : base + 64, :].astype(F32)[8:]
            middle = table_ref[map_ref[slot, tap + 3], base : base + 64, :].astype(F32)
            after = table_ref[map_ref[slot, tap + 6], base : base + 16, :].astype(F32)[:8]
            spans.append(jnp.concatenate((before, middle, after), axis=0).reshape(EDGE + 2, EDGE, CH))
        low, centre, high = spans
        down = pltpu.roll(jnp.where(sub == EDGE - 1, low, centre), 1, 1)
        up = pltpu.roll(jnp.where(sub == 0, high, centre), EDGE - 1, 1)
        for r, source in ((-1, down), (0, centre), (1, up)):
            for q in (-1, 0, 1):
                rows = source[q + 1 : q + 1 + EDGE].reshape(PLANE, CH).astype(BF16)
                lane = (3 * (q + 1) + r + 1) * CH
                x9_ref[(a + 1) * PLANE : (a + 2) * PLANE, lane : lane + CH] = rows


def fill_whole(table_ref, refs):
    start = 0
    for ref in refs:
        table_ref[start : start + ref.shape[0]] = ref[...]
        start += ref.shape[0]


def fill_faces(table_ref, refs):
    own_ref, xl_ref, xu_ref, yl_ref, yu_ref = refs
    table_ref[0:SLOTS] = own_ref[...]
    for k in range(HX):
        table_ref[SLOTS + k, VOX - PLANE : VOX, :] = xl_ref[k]
        table_ref[SLOTS + HX + k, 0:PLANE, :] = xu_ref[k]
    empty = jnp.zeros((EDGE, CH), F32)
    first = SLOTS + 2 * HX
    for k in range(HY):
        low = yl_ref[k * PLANE : (k + 1) * PLANE, :].astype(F32)
        high = yu_ref[k * PLANE : (k + 1) * PLANE, :].astype(F32)
        for a in range(EDGE):
            part = slice(a * EDGE, (a + 1) * EDGE)
            base = a * PLANE
            table_ref[first + k, base + 48 : base + 64, :] = jnp.concatenate(
                (empty, low[part]), axis=0
            ).astype(BF16)
            table_ref[first + HY + k, base : base + 16, :] = jnp.concatenate(
                (high[part], empty), axis=0
            ).astype(BF16)


def count_misfits(rows, yl_ref, yu_ref):
    lane = lax.broadcasted_iota(jnp.int32, rows.shape, 1)
    within = lane - jnp.where(lane >= 9, 9, 0) - jnp.where(lane >= 18, 9, 0)
    not_down, not_up = lane >= 9, lane < 18
    bad = (rows >= SLOTS) & (rows < SLOTS + HX) & not_down
    bad = bad | ((rows >= SLOTS + HX) & (rows < SLOTS + 2 * HX) & not_up)
    for start, ref, wrong in (
        (SLOTS + 2 * HX, yl_ref, within >= 3),
        (SLOTS + 2 * HX + HY, yu_ref, within < 6),
    ):
        origin = ref[HY * PLANE : FACE_ROWS, :].astype(F32)
        for k in range(HY):
            code = jnp.broadcast_to(origin[k : k + 1, 0 : rows.shape[1]], rows.shape)
            fault = wrong | ((code == 1.0) & not_down) | ((code == 2.0) & not_up)
            bad = bad | ((rows == start + k) & fault)
    return jnp.sum(jnp.where(bad, 1.0, 0.0))


def conv_kernel(
    map_ref, rows_ref, own_ref, xl_ref, xu_ref, yl_ref, yu_ref, w_ref, mask_ref,
    out_ref, x9_out, stat_ref, table_ref, x9_ref, sems,
):
    fill_faces(table_ref, (own_ref, xl_ref, xu_ref, yl_ref, yu_ref))
    table_ref[16] = jnp.zeros((VOX, CH), BF16)
    sums = [jnp.zeros((1, CH), F32)] * 3
    copies = []

    def columns(slot):
        fill_columns(map_ref, slot, table_ref, x9_ref.at[slot])
        copies.append(pltpu.make_async_copy(x9_ref.at[slot], x9_out.at[slot], sems.at[slot]))
        copies[-1].start()

    columns(0)
    for slot in range(SLOTS):
        if slot + 1 < SLOTS:
            columns(slot + 1)
        total = None
        for p in range(3):
            term = jnp.dot(
                x9_ref[slot, p * PLANE : p * PLANE + VOX, :], w_ref[p], preferred_element_type=F32
            )
            total = term if total is None else total + term
        mask = mask_ref[slot].astype(F32)
        masked = total * mask
        out_ref[slot] = total
        terms = (masked, masked * total, mask)
        sums = [s + jnp.sum(term, axis=0, keepdims=True) for s, term in zip(sums, terms)]
    misfits = count_misfits(rows_ref[...], yl_ref, yu_ref)
    sums.append(jnp.broadcast_to(misfits, (1, CH)))
    stat_ref[...] = jnp.concatenate(sums + [jnp.zeros((4, CH), F32)], axis=0)
    for copy in copies:
        copy.wait()


def conv(row_map, own, xl, xu, yl, yu, weight, mask):
    columns = (SLOTS, 10 * PLANE, 9 * CH)
    return pl.pallas_call(
        conv_kernel,
        out_shape=(shape((SLOTS, VOX, CH), F32), shape(columns, BF16), shape((8, CH), F32)),
        in_specs=[SM] + [VM] * 8,
        out_specs=(VM, pl.BlockSpec(memory_space=pl.ANY), VM),
        scratch_shapes=[
            pltpu.VMEM((17, VOX, CH), BF16),
            pltpu.VMEM(columns, BF16),
            pltpu.SemaphoreType.DMA((SLOTS,)),
        ],
        compiler_params=params(28),
        cost_estimate=cost(6000000000, 12 << 20),
        name="forward_conv",
    )(row_map, row_map, own, xl, xu, yl, yu, weight, mask)


def step_kernel(
    map_ref, rows_ref, own_ref, xl_ref, xu_ref, yl_ref, yu_ref, w_ref, mask_ref, *rest, forward, faces
):
    slot = pl.program_id(0)
    if forward:
        out_ref, x9_out, stat_ref, table_ref = rest
        x9_ref = x9_out.at[0]
    else:
        out_ref, table_ref, x9_ref = rest

    @pl.when(slot == 0)
    def _():
        fill = fill_faces if faces else fill_whole
        fill(table_ref, (own_ref, xl_ref, xu_ref, yl_ref, yu_ref))
        table_ref[16] = jnp.zeros((VOX, CH), BF16)
        if forward:
            stat_ref[...] = jnp.zeros_like(stat_ref)
            if faces:
                stat_ref[3:4] = jnp.broadcast_to(
                    count_misfits(rows_ref[...], yl_ref, yu_ref), (1, CH)
                )

    fill_columns(map_ref, slot, table_ref, x9_ref)
    total = None
    for p in range(3):
        term = jnp.dot(
            x9_ref[p * PLANE : p * PLANE + VOX, :], w_ref[p], preferred_element_type=F32
        )
        total = term if total is None else total + term
    mask = mask_ref[0].astype(F32)
    masked = total * mask
    if forward:
        out_ref[0] = total
        stat_ref[0:1] += jnp.sum(masked, axis=0, keepdims=True)
        stat_ref[1:2] += jnp.sum(masked * total, axis=0, keepdims=True)
        stat_ref[2:3] += jnp.sum(mask, axis=0, keepdims=True)
    else:
        out_ref[0] = masked.astype(BF16)


def whole(*dims):
    return pl.BlockSpec(dims, lambda s: (0,) * len(dims))


def conv_steps(row_map, own, xl, xu, yl, yu, weight, mask, forward, faces):
    brick = pl.BlockSpec((1, VOX, CH), lambda s: (s, 0, 0))
    scratch = [pltpu.VMEM((17, VOX, CH), BF16)]
    if forward:
        out_shape = (
            shape((SLOTS, VOX, CH), F32),
            shape((SLOTS, 10 * PLANE, 9 * CH), BF16),
            shape((8, CH), F32),
        )
        out_specs = (brick, pl.BlockSpec((1, 10 * PLANE, 9 * CH), lambda s: (s, 0, 0)), whole(8, CH))
    else:
        out_shape = shape((SLOTS, VOX, CH), BF16)
        out_specs = brick
        scratch.append(pltpu.VMEM((10 * PLANE, 9 * CH), BF16))
    return pl.pallas_call(
        functools.partial(step_kernel, forward=forward, faces=faces),
        grid=(SLOTS,),
        out_shape=out_shape,
        in_specs=[
            SM,
            whole(*row_map.shape),
            whole(*own.shape),
            whole(*xl.shape),
            whole(*xu.shape),
            whole(*yl.shape),
            whole(*yu.shape),
            whole(3, 9 * CH, CH),
            brick,
        ],
        out_specs=out_specs,
        scratch_shapes=scratch,
        compiler_params=params(24),
        cost_estimate=cost(6000000000, 12 << 20),
        name="forward_steps" if forward else "transposed_conv",
    )(row_map, row_map, own, xl, xu, yl, yu, weight, mask)


def norm_terms(stats):
    count = stats[2:3]
    mean = stats[0:1] / count
    variance = stats[1:2] / count - mean * mean
    return count, mean, lax.rsqrt(variance + EPSILON)


def activate(slot, stats, cot_ref, conv_ref, mask_ref, gain_ref, shift_ref, act_ref, ga_ref, g_ref):
    count, mean, inverse = stats
    mask = mask_ref[slot].astype(F32)
    normed = (conv_ref[slot] - mean) * inverse
    pre = gain_ref[...] * normed + shift_ref[...]
    sig = jax.nn.sigmoid(pre)
    act_ref[slot] = (pre * sig * mask).astype(BF16)
    ga = cot_ref[slot].astype(F32) * mask * sig * (1.0 + pre * (1.0 - sig))
    ga_ref[slot] = ga
    nm = normed * mask
    for k in range(VOX // CH):
        rows = slice(k * CH, (k + 1) * CH)
        g_ref[slot, 0:CH, rows] = jnp.transpose(ga[rows]).astype(BF16)
        g_ref[slot, CH : 2 * CH, rows] = jnp.transpose(nm[rows]).astype(BF16)
        g_ref[slot, 2 * CH : 2 * CH + 16, rows] = jnp.transpose(mask[rows])[0:16].astype(BF16)
    sums = (jnp.sum(ga, axis=0, keepdims=True), jnp.sum(ga * normed, axis=0, keepdims=True))
    return jnp.concatenate(sums, axis=0)


def split(value, pieces):
    parts = []
    for _ in range(pieces):
        part = value.astype(BF16).astype(F32)
        parts.append(part)
        value = value - part
    return parts


def pack(ones, sums):
    parts = split(ones, 2) + split(sums[0:1], 3) + split(sums[1:2], 3)
    used = sum(part.shape[0] for part in parts)
    rows = -(-used // 16) * 16
    if used < rows:
        parts.append(jnp.zeros((rows - used, CH), F32))
    return jnp.concatenate(parts, axis=0).astype(BF16)


def unpack(rows, taps):
    ones = rows[0:taps] + rows[taps : 2 * taps]
    at = 2 * taps
    first = rows[at : at + 1] + rows[at + 1 : at + 2] + rows[at + 2 : at + 3]
    second = rows[at + 3 : at + 4] + rows[at + 4 : at + 5] + rows[at + 5 : at + 6]
    return ones, jnp.concatenate((first, second), axis=0)


def wgrad_kernel(
    core_ref, stat_ref, conv_ref, cot_ref, mask_ref, gain_ref, shift_ref, x9_hbm,
    act_ref, ga_ref, norm_ref, keep_ref, send_ref, g_ref, x9_ref, hold_ref, sems, *, unroll
):
    copies = [
        pltpu.make_async_copy(x9_hbm.at[s], x9_ref.at[s], sems.at[s]) for s in range(SLOTS)
    ]
    for copy in copies:
        copy.start()
    stats = norm_terms(jnp.sum(stat_ref[...], axis=0))
    count, mean, inverse = stats
    norm_ref[...] = jnp.concatenate((mean, inverse, count, jnp.zeros((5, CH), F32)), axis=0)

    def add_sums(s, sums):
        return sums + activate(
            s, stats, cot_ref, conv_ref, mask_ref, gain_ref, shift_ref, act_ref, ga_ref, g_ref
        )

    sums = lax.fori_loop(0, SLOTS, add_sums, jnp.zeros((2, CH), F32), unroll=unroll)
    for copy in copies:
        copy.wait()
    ones = [None] * 27
    for p in range(3):
        for q in range(0, 9, 2):
            width = min(2, 9 - q)
            lanes = slice(q * CH, (q + width) * CH)

            def add_term(s, total):
                rows = slice(p * PLANE, p * PLANE + VOX)
                return total + jnp.dot(
                    g_ref[s], x9_ref[s, rows, lanes], preferred_element_type=F32
                )

            if unroll:
                total = None
                for s in range(SLOTS):
                    total = add_term(s, 0.0 if total is None else total)
            else:
                empty = jnp.zeros((2 * CH + 16, width * CH), F32)
                total = lax.fori_loop(0, SLOTS, add_term, empty)
            for r in range(width):
                t = 9 * p + q + r
                tap = total[:, r * CH : (r + 1) * CH]
                ones[t] = tap[2 * CH : 2 * CH + 1]
                for half in (0, 1):
                    i = t - 13 * half
                    if 0 <= i < 14:
                        for k in range(16):
                            pair = jnp.concatenate(
                                (tap[8 * k : 8 * k + 8], tap[CH + 8 * k : CH + 8 * k + 8]), axis=0
                            )
                            row = k * MAIN + i * 16
                            hold_ref[half, row : row + 16, :] = pair
    for half in (0, 1):
        rows = jnp.concatenate(ones[13 * half : 13 * half + 14], axis=0)
        hold_ref[half, 16 * MAIN : 16 * MAIN + EXTRA, :] = pack(rows, sums).astype(F32)
    core = core_ref[0]
    keep_ref[...] = hold_ref[core]
    send_ref[...] = hold_ref[1 - core].astype(BF16)


def wgrad(core, stats, conv_out, cotangent, mask, gain, shift, x9, unroll):
    rows = 16 * MAIN + EXTRA
    return pl.pallas_call(
        functools.partial(wgrad_kernel, unroll=unroll),
        out_shape=(
            shape((SLOTS, VOX, CH), BF16),
            shape((SLOTS, VOX, CH), F32),
            shape((8, CH), F32),
            shape((rows, CH), F32),
            shape((rows, CH), BF16),
        ),
        in_specs=[SM] + [VM] * 6 + [pl.BlockSpec(memory_space=pl.ANY)],
        out_specs=(VM,) * 5,
        scratch_shapes=[
            pltpu.VMEM((SLOTS, 2 * CH + 16, VOX), BF16),
            pltpu.VMEM((SLOTS, 10 * PLANE, 9 * CH), BF16),
            pltpu.VMEM((2, rows, CH), F32),
            pltpu.SemaphoreType.DMA((SLOTS,)),
        ],
        compiler_params=params(28),
        cost_estimate=cost(6000000000, 12 << 20),
        name="weight_terms",
    )(core, stats, conv_out, cotangent, mask, gain, shift, x9)


def join_kernel(keep_ref, got_ref, out_ref):
    for k in range(16):
        rows = slice(k * MAIN, (k + 1) * MAIN)
        out_ref[k, 0:MAIN, :] = (keep_ref[rows, :] + got_ref[rows, :].astype(F32)).astype(BF16)
    rows = slice(16 * MAIN, 16 * MAIN + EXTRA)
    ones, sums = unpack(keep_ref[rows, :], 14)
    more_ones, more_sums = unpack(got_ref[rows, :].astype(F32), 14)
    extra = pack(ones + more_ones, sums + more_sums)
    for k in range(16):
        out_ref[k, MAIN : MAIN + EXTRA, :] = extra


def join(keep, got):
    return pl.pallas_call(
        join_kernel,
        out_shape=shape((16, MAIN + EXTRA, CH), BF16),
        in_specs=[VM, VM],
        out_specs=VM,
        compiler_params=params(),
        cost_estimate=cost(1 << 20, 3 << 20),
        name="join",
    )(keep, got)


def middle_kernel(parts_ref, out_ref):
    extra = None
    for k in range(16):
        ones, sums = unpack(parts_ref[k, MAIN : MAIN + EXTRA, :].astype(F32), 14)
        extra = (ones, sums) if extra is None else (extra[0] + ones, extra[1] + sums)
    for z in range(8):
        if z < 7:
            total = None
            for k in range(16):
                term = parts_ref[k, 32 * z : 32 * (z + 1), :].astype(F32)
                total = term if total is None else total + term
            ones = extra[0][2 * z : 2 * z + 2]
        else:
            total, ones = jnp.zeros((32, CH), F32), jnp.zeros((2, CH), F32)
        out_ref[z] = jnp.concatenate((total, ones, extra[1], jnp.zeros((4, CH), F32)), axis=0)


def middle(parts):
    return pl.pallas_call(
        middle_kernel,
        out_shape=shape((8, 40, CH), F32),
        in_specs=[VM],
        out_specs=VM,
        compiler_params=params(),
        cost_estimate=cost(1 << 20, 2 << 20),
        name="middle",
    )(parts)


def column(row):
    return jnp.transpose(jnp.broadcast_to(row, (CH, CH)))


def combine_kernel(block_ref, parts_ref, norm_ref, gain_ref, out_ref, gg_ref, sg_ref, coef_ref):
    total = jnp.sum(parts_ref[...], axis=0)
    main, ones, sums = total[0:32], total[32:34], total[34:36]
    inverse, count = norm_ref[1:2], norm_ref[2:3]
    scale = lax.rsqrt(count)
    sg_ref[...] = sums[0:1] * scale
    gg_ref[...] = sums[1:2] * scale
    coef_ref[0] = column(gain_ref[...] * inverse * scale)
    coef_ref[1] = column(sums[0:1] / count)
    coef_ref[2] = column(sums[1:2] / count)
    mine = pl.ds(pl.multiple_of(block_ref[0] * 8, 8), 8)
    factor, first, second = coef_ref[0, mine, :], coef_ref[1, mine, :], coef_ref[2, mine, :]
    values = []
    for i in range(2):
        base, cross = main[16 * i : 16 * i + 8], main[16 * i + 8 : 16 * i + 16]
        values.append(factor * (base - first * ones[i : i + 1] - second * cross))
    out_ref[...] = jnp.concatenate(values, axis=0).astype(BF16)


def combine(block, parts, norm, gain):
    return pl.pallas_call(
        combine_kernel,
        out_shape=(shape((16, CH), BF16), shape((1, CH), F32), shape((1, CH), F32)),
        in_specs=[SM] + [VM] * 3,
        out_specs=(VM,) * 3,
        scratch_shapes=[pltpu.VMEM((3, CH, CH), F32)],
        compiler_params=params(),
        cost_estimate=cost(1 << 20, 1 << 20),
        name="combine",
    )(block, parts, norm, gain)


def grad_kernel(
    sends_ref, parts_ref, norm_ref, gain_ref, conv_ref, ga_ref, mask_ref, out_ref, low_ref, high_ref, *, faces
):
    totals = jnp.sum(parts_ref[...], axis=0)[34:36]
    mean, inverse, count = norm_ref[0:1], norm_ref[1:2], norm_ref[2:3]
    factor = gain_ref[...] * inverse
    for s in range(SLOTS):
        normed = (conv_ref[s] - mean) * inverse
        inner = ga_ref[s] - (totals[0:1] + normed * totals[1:2]) / count
        out_ref[s] = (factor * inner * mask_ref[s].astype(F32)).astype(BF16)
    pick_x(sends_ref, out_ref, low_ref, high_ref, faces)


def grad(sends_x, parts, norm, gain, conv_out, ga, mask, faces):
    return pl.pallas_call(
        functools.partial(grad_kernel, faces=faces),
        out_shape=(shape((SLOTS, VOX, CH), BF16),) + x_shapes(faces),
        in_specs=[SM] + [VM] * 6,
        out_specs=(VM,) * 3,
        compiler_params=params(),
        cost_estimate=cost(4 << 20, 4 << 20),
        name="grad_conv",
    )(sends_x, parts, norm, gain, conv_out, ga, mask)


def finish_kernel(core_ref, mine_ref, other_ref, out_ref):
    for half in (0, 1):
        here = core_ref[0] == half
        for z in range(7):
            pairs = []
            for k in range(16):
                rows = slice(16 * z, 16 * (z + 1))
                pairs.append(jnp.where(here, mine_ref[k, rows, :], other_ref[k, rows, :]).astype(F32))
            for i in range(2):
                tap = 13 * half + 2 * z + i
                if half == 1 and tap == 13:
                    continue
                rows = jnp.concatenate([pair[8 * i : 8 * i + 8] for pair in pairs], axis=0)
                out_ref[tap] = jnp.transpose(rows)


def finish(core, mine, other):
    return pl.pallas_call(
        finish_kernel,
        out_shape=shape((27, CH, CH), F32),
        in_specs=[SM, VM, VM],
        out_specs=VM,
        compiler_params=params(),
        cost_estimate=cost(1 << 20, 3 << 20),
        name="finish",
    )(core, mine, other)


def spread(value, axes):
    size = axis_size(axes)
    return lax.all_to_all(jnp.broadcast_to(value[None], (size,) + value.shape), axes, 0, 0)


def all_sum_parts(value):
    return spread(jnp.sum(spread(value, ("z", "c")), axis=0), CROSS)


def swap(value):
    return lax.ppermute(value, "c", [(0, 1), (1, 0)])


def turn_kernel(w_ref, out_ref):
    for t in range(27):
        rows = slice((t % 9) * CH, (t % 9 + 1) * CH)
        out_ref[t // 9, rows, :] = jnp.transpose(w_ref[26 - t].astype(F32)).astype(BF16)


def turn(weight):
    return pl.pallas_call(
        turn_kernel,
        out_shape=shape((3, 9 * CH, CH), BF16),
        in_specs=[VM],
        out_specs=VM,
        compiler_params=params(),
        cost_estimate=cost(1 << 20, 2 << 20),
        name="turn",
    )(weight)


def shards(
    features,
    occupancy,
    counts,
    kernel_map,
    x_send,
    y_send,
    weight,
    norm_gain,
    norm_shift,
    cotangent,
):
    row_map, sends_x, sends_y = kernel_map[0, 0], x_send[0, 0], y_send[0, 0]
    gain, shift = norm_gain.reshape(1, CH), norm_shift.reshape(1, CH)
    core = lax.axis_index("c").reshape(1)
    block = lax.axis_index(CROSS).reshape(1)
    ahead = weight.reshape(3, 9 * CH, CH)

    def first(faces):
        own, mask, low, high = prepare(counts, sends_x, features[0, 0], occupancy[0, 0], faces)
        later, low, high = lax.optimization_barrier((weight, low, high))
        xl, xu = neighbours(low, high, ("xh", "y"))
        xl, xu, turned = lax.optimization_barrier((xl, xu, turn(later)))
        low, high = pick_y(sends_y, own, xl, xu, faces)
        yl, yu = neighbours(low, high, ("xl", "z", "c"))
        table = (row_map, own, xl, xu, yl, yu, ahead, mask)
        conv_out, x9, stats = conv(*table) if faces else conv_steps(*table, True, False)
        return conv_out, x9, mask, turned, all_sum_parts(stats)

    def second(conv_out, x9, mask, turned, stats, faces):
        activations, ga, norm, keep, send = wgrad(
            core, stats, conv_out, cotangent[0, 0], mask, gain, shift, x9, faces
        )
        parts = lax.all_to_all(join(keep, swap(send)), CROSS, 0, 0)
        parts = lax.all_to_all(middle(parts), "z", 0, 0)
        grads, low, high = grad(sends_x, parts, norm, gain, conv_out, ga, mask, faces)
        parts, low, high = lax.optimization_barrier((parts, low, high))
        xl, xu = neighbours(low, high, ("xh", "y"))
        value, gain_grad, shift_grad = combine(block, parts, norm, gain)
        mine = spread(value, ("z",)).reshape(8 * 16, CH)[: 7 * 16]
        low, high = pick_y(sends_y, grads, xl, xu, faces)
        mine, low, high = lax.optimization_barrier((mine, low, high))
        yl, yu = neighbours(low, high, ("xl", "z", "c"))
        mine = spread(mine, CROSS)
        features_grad = conv_steps(row_map, grads, xl, xu, yl, yu, turned, mask, False, faces)
        mine, features_grad = lax.optimization_barrier((mine, features_grad))
        weight_grad = finish(core, mine, swap(mine))
        return activations, features_grad, weight_grad, gain_grad, shift_grad

    state = first(True)
    misfits = jnp.sum(state[4][:, 3, 0])
    activations, features_grad, weight_grad, gain_grad, shift_grad = lax.cond(
        misfits > 0,
        lambda *_: second(*first(False), False),
        lambda *given: second(*given, True),
        *state,
    )
    return (
        activations[None, None],
        features_grad[None, None],
        weight_grad,
        gain_grad.reshape(CH),
        shift_grad.reshape(CH),
    )


def solution(mesh):
    fine = jax.sharding.Mesh(mesh.devices.reshape(2, 4, 2, 8, 2), ("xh", "y", "xl", "z", "c"))
    gx, gy = ("xh", "y"), ("xl", "z", "c")
    tiles = P(gx, gy, None, None, None)
    lists = P(gx, gy, None, None)
    return jax.shard_map(
        shards,
        mesh=fine,
        in_specs=(tiles, lists, P(gx, gy), lists, lists, lists, P(), P(), P(), tiles),
        out_specs=(tiles, tiles, P(), P(), P()),
        check_vma=False,
    )
```

profile of v0, /device:TPU:1, one launch (start us, length us, event | category | flops | bytes accessed | tf_op | source)
XLA Modules:
  0.0 154.4 jit_solution(464369891576517571)
XLA Ops:
  0.6 0.0 copy-start.2
  1.4 1.4 prepare.3
  2.8 4.0 %collective-permute-start.16 = (bf16[2,64,128]{2,1,0:T(8,128)(2,1)S(1)}, bf16[2,64,128]{2,1,0:T(8,128)(2,1)S(1)}, u32[]{:S(2)}, u32[]{:S(2)}) collective-permute-start(bf16[2,64,128]{2,1,0:T(8,128)(2,1)S(1)} %get-tuple-element.163), channel_id=1, source_target_pairs={{0,32},{32,64},{64,96},{96,128},{128,160},{160,192},{192,224},{1,3... | collective-permute-start | bytes 98312 | tf_op jit(solution)/shard_map/ppermute | solution.py:174
  6.8 1.3 collective-permute-start.17
  8.1 2.4 %turn.3 = bf16[3,1152,128]{2,1,0:T(8,128)(2,1)} custom-call(bf16[27,128,128]{2,1,0:T(8,128)(2,1)} %w_ref), custom_call_target="tpu_custom_call" | custom-call | flops 1048576 | bytes 2097152 | tf_op jit(solution)/shard_map/turn/pallas_call | solution.py:681
  10.5 1.0 collective-permute-done.17.xu_ref
  11.5 0.7 pick_y.7
  12.3 5.5 %collective-permute-start.18 = (bf16[272,128]{1,0:T(8,128)(2,1)S(1)}, bf16[272,128]{1,0:T(8,128)(2,1)S(1)}, u32[]{:S(2)}, u32[]{:S(2)}) collective-permute-start(bf16[272,128]{1,0:T(8,128)(2,1)S(1)} %get-tuple-element.168), channel_id=1, source_target_pairs={{0,1},{1,2},{2,3},{3,4},{4,5},{5,6},{6,7},{7,8},{8,9},{9,10},{10,1... | collective-permute-start | bytes 208904 | tf_op jit(solution)/shard_map/ppermute | solution.py:174
  17.8 1.9 %collective-permute-start.19 = (bf16[272,128]{1,0:T(8,128)(2,1)S(1)}, bf16[272,128]{1,0:T(8,128)(2,1)S(1)}, u32[]{:S(2)}, u32[]{:S(2)}) collective-permute-start(bf16[272,128]{1,0:T(8,128)(2,1)S(1)} %get-tuple-element.169), channel_id=1, source_target_pairs={{1,0},{2,1},{3,2},{4,3},{5,4},{6,5},{7,6},{8,7},{9,8},{10,9},{11,1... | collective-permute-start | bytes 208904 | tf_op jit(solution)/shard_map/ppermute | solution.py:174
  19.7 3.7 %collective-permute-done.19.yu_ref = bf16[272,128]{1,0:T(8,128)(2,1)S(1)} collective-permute-done((bf16[272,128]{1,0:T(8,128)(2,1)S(1)}, bf16[272,128]{1,0:T(8,128)(2,1)S(1)}, u32[]{:S(2)}, u32[]{:S(2)}) %collective-permute-start.19) | collective-permute-done | bytes 69664 | tf_op jit(solution)/shard_map/ppermute | solution.py:174
  23.4 0.0 copy-start.10
  23.4 0.0 copy-start.12
  23.5 0.0 copy-start.15
  23.5 5.7 %forward_conv.1 = (f32[4,512,128]{2,1,0:T(8,128)S(1)}, bf16[4,640,1152]{2,1,0:T(8,128)(2,1)}, f32[8,128]{1,0:T(8,128)S(1)}) custom-call(s32[4,27]{1,0:T(4,128)S(1)} %bitcast.39, s32[4,27]{1,0:T(4,128)S(1)} %bitcast.40, bf16[4,512,128]{2,1,0:T(8,128)(2,1)S(1)} %get-tuple-element.160.own_ref, bf16[2,64,128]{2,1,0:T(8,128)(2,1)S(1)} %collective-permute-done.16.xl_ref, ...), custom_call_target="tpu_custom_call" | custom-call | flops 6000000000 | bytes 12582912 | tf_op jit(solution)/shard_map/forward_conv/pallas_call | solution.py:284
  29.1 16.0 %all_to_all.57 = f32[16,8,128]{2,1,0:T(8,128)S(1)} all-to-all(f32[16,8,128]{2,1,0:T(8,128)S(1)} %broadcast_in_dim.28), channel_id=1, replica_groups=mesh['xh'=2,'y'=4,'xl'=2,'z'=8,'c'=2] {'z','c'}, dimensions={0} | all-to-all | bytes 131072 | tf_op jit(solution)/shard_map/all_to_all | solution.py:663
  45.2 0.6 broadcast_in_dim.29
  45.8 8.9 %all-to-all-start.11 = ((f32[16,8,128]{2,1,0:T(8,128)}), f32[16,8,128]{2,1,0:T(8,128)S(1)}, u32[]{:S(2)}, u32[]{:S(2)}) async-start(f32[16,8,128]{2,1,0:T(8,128)} %broadcast_in_dim.29), calls=%async_computation.11 | async-start | bytes 131072 | tf_op jit(solution)/shard_map/all_to_all | solution.py:663
  54.7 6.5 %all-to-all-done.11 = f32[16,8,128]{2,1,0:T(8,128)S(1)} async-done(((f32[16,8,128]{2,1,0:T(8,128)}), f32[16,8,128]{2,1,0:T(8,128)S(1)}, u32[]{:S(2)}, u32[]{:S(2)}) %all-to-all-start.11) | async-done | bytes 65568 | tf_op jit(solution)/shard_map/all_to_all | solution.py:663
  61.2 0.6 slice_reduce_fusion
  62.6 90.7 %conditional.1 = (bf16[4,512,128]{2,1,0:T(8,128)(2,1)}, bf16[4,512,128]{2,1,0:T(8,128)(2,1)}, f32[27,128,128]{2,1,0:T(8,128)S(1)}, f32[1,128]{1,0:T(1,128)}, f32[1,128]{1,0:T(1,128)}) conditional(s32[]{:T(128)} %convert_element_type.3, (bf16[1,1,4,512,128]{4,3,2,1,0:T(8,128)(2,1)}, s32[1]{0:T(128)}, f32[16,8,128]{2,1,0:T(8,128)S(1)}, ...), branch_computations={%region_2.0_spmd, %region_3.0_spmd} | conditional | flops 18012598272 | bytes 135778880 | solution.py:743
  62.6 0.0 copy-start.7
  62.6 9.3 %weight_terms.2 = (bf16[4,512,128]{2,1,0:T(8,128)(2,1)}, f32[4,512,128]{2,1,0:T(8,128)S(1)}, f32[8,128]{1,0:T(8,128)S(1)}, f32[3632,128]{1,0:T(8,128)S(1)}, bf16[3632,128]{1,0:T(8,128)(2,1)S(1)}) custom-call(s32[1]{0:T(128)} %get-tuple-element.52.core_ref, f32[16,8,128]{2,1,0:T(8,128)S(1)} %get-tuple-element.53.stat_ref, ...), custom_call_target="tpu_custom_call" | custom-call | flops 6000000000 | bytes 12582912 | tf_op jit(solution)/shard_map/cond/branch_0_fun/weight_terms/pallas_call | solution.py:496
  71.9 1.7 %collective-permute-start = (bf16[3632,128]{1,0:T(8,128)(2,1)S(1)}, bf16[3632,128]{1,0:T(8,128)(2,1)S(1)}, u32[]{:S(2)}, u32[]{:S(2)}) collective-permute-start(bf16[3632,128]{1,0:T(8,128)(2,1)S(1)} %get-tuple-element.63), channel_id=1, source_target_pairs={{0,1},{1,0},{2,3},{3,2},{4,5},{5,4},{6,7},{7,6},{8,9},{9,8},{10,11... | collective-permute-start | bytes 2789384 | tf_op jit(solution)/shard_map/cond/branch_0_fun/ppermute | solution.py:671
  73.5 2.1 %collective-permute-done.got_ref = bf16[3632,128]{1,0:T(8,128)(2,1)S(1)} collective-permute-done((bf16[3632,128]{1,0:T(8,128)(2,1)S(1)}, bf16[3632,128]{1,0:T(8,128)(2,1)S(1)}, u32[]{:S(2)}, u32[]{:S(2)}) %collective-permute-start) | collective-permute-done | bytes 929824 | tf_op jit(solution)/shard_map/cond/branch_0_fun/ppermute | solution.py:671
  75.7 0.2 join.2
  75.9 0.0 copy-start.8
  75.9 20.2 %all_to_all.50.parts_ref = bf16[16,272,128]{2,1,0:T(8,128)(2,1)S(1)} all-to-all(bf16[16,272,128]{2,1,0:T(8,128)(2,1)S(1)} %join.2), channel_id=1, replica_groups=mesh['xh'=2,'y'=4,'xl'=2,'z'=8,'c'=2] {'xh','y','xl'}, dimensions={0} | all-to-all | bytes 2228224 | tf_op jit(solution)/shard_map/cond/branch_0_fun/all_to_all | solution.py:725
  96.1 0.2 middle.2
  96.3 10.8 %all_to_all.51.parts_ref = f32[8,40,128]{2,1,0:T(8,128)S(1)} all-to-all(f32[8,40,128]{2,1,0:T(8,128)S(1)} %middle.2), channel_id=1, replica_groups=mesh['xh'=2,'y'=4,'xl'=2,'z'=8,'c'=2] {'z'}, dimensions={0} | all-to-all | bytes 327680 | tf_op jit(solution)/shard_map/cond/branch_0_fun/all_to_all | solution.py:726
  107.1 1.1 grad_conv.2
  108.2 0.5 combine.2
  108.7 0.6 broadcast_in_dim.6
  109.3 3.3 %all-to-all-start.2 = ((bf16[8,16,128]{2,1,0:T(8,128)(2,1)}), bf16[8,16,128]{2,1,0:T(8,128)(2,1)S(1)}, u32[]{:S(2)}, u32[]{:S(2)}) async-start(bf16[8,16,128]{2,1,0:T(8,128)(2,1)} %broadcast_in_dim.6), calls=%async_computation.2 | async-start | bytes 65536 | tf_op jit(solution)/shard_map/cond/branch_0_fun/all_to_all | solution.py:663
  112.7 1.8 %collective-permute-start.1 = (bf16[2,64,128]{2,1,0:T(8,128)(2,1)S(1)}, bf16[2,64,128]{2,1,0:T(8,128)(2,1)S(1)}, u32[]{:S(2)}, u32[]{:S(2)}) collective-permute-start(bf16[2,64,128]{2,1,0:T(8,128)(2,1)S(1)} %get-tuple-element.73), channel_id=1, source_target_pairs={{0,32},{32,64},{64,96},{96,128},{128,160},{160,192},{192,224},{1,3... | collective-permute-start | bytes 98312 | tf_op jit(solution)/shard_map/cond/branch_0_fun/ppermute | solution.py:174
  114.5 1.3 collective-permute-start.2
  115.8 3.6 %collective-permute-done.2.xu_ref = bf16[2,64,128]{2,1,0:T(8,128)(2,1)S(1)} collective-permute-done((bf16[2,64,128]{2,1,0:T(8,128)(2,1)S(1)}, bf16[2,64,128]{2,1,0:T(8,128)(2,1)S(1)}, u32[]{:S(2)}, u32[]{:S(2)}) %collective-permute-start.2) | collective-permute-done | bytes 32800 | tf_op jit(solution)/shard_map/cond/branch_0_fun/ppermute | solution.py:174
  119.4 0.7 pick_y.4
  120.2 7.5 %collective-permute-start.3 = (bf16[272,128]{1,0:T(8,128)(2,1)S(1)}, bf16[272,128]{1,0:T(8,128)(2,1)S(1)}, u32[]{:S(2)}, u32[]{:S(2)}) collective-permute-start(bf16[272,128]{1,0:T(8,128)(2,1)S(1)} %get-tuple-element.79), channel_id=1, source_target_pairs={{0,1},{1,2},{2,3},{3,4},{4,5},{5,6},{6,7},{7,8},{8,9},{9,10},{10,1... | collective-permute-start | bytes 208904 | tf_op jit(solution)/shard_map/cond/branch_0_fun/ppermute | solution.py:174
  127.7 1.9 %collective-permute-start.4 = (bf16[272,128]{1,0:T(8,128)(2,1)S(1)}, bf16[272,128]{1,0:T(8,128)(2,1)S(1)}, u32[]{:S(2)}, u32[]{:S(2)}) collective-permute-start(bf16[272,128]{1,0:T(8,128)(2,1)S(1)} %get-tuple-element.80), channel_id=1, source_target_pairs={{1,0},{2,1},{3,2},{4,3},{5,4},{6,5},{7,6},{8,7},{9,8},{10,9},{11,1... | collective-permute-start | bytes 208904 | tf_op jit(solution)/shard_map/cond/branch_0_fun/ppermute | solution.py:174
  129.7 0.8 broadcast_in_dim.7
  130.5 8.3 %all-to-all-start.3 = ((bf16[16,112,128]{2,1,0:T(8,128)(2,1)}), bf16[16,112,128]{2,1,0:T(8,128)(2,1)S(1)}, u32[]{:S(2)}, u32[]{:S(2)}) async-start(bf16[16,112,128]{2,1,0:T(8,128)(2,1)} %broadcast_in_dim.7), calls=%async_computation.3 | async-start | bytes 917504 | tf_op jit(solution)/shard_map/cond/branch_0_fun/all_to_all | solution.py:663
  138.9 6.0 %transposed_conv.2 = bf16[4,512,128]{2,1,0:T(8,128)(2,1)} custom-call(s32[4,27]{1,0:T(4,128)S(1)} %get-tuple-element.78.map_ref.rows_ref, s32[4,27]{1,0:T(4,128)S(1)} %get-tuple-element.78.map_ref.rows_ref, bf16[4,512,128]{2,1,0:T(8,128)(2,1)S(1)} %get-tuple-element.72.own_ref, bf16[2,64,128]{2,1,0:T(8,128)(2,1)S(1)} %collective-permute-done.1.xl_ref, ...), custom_call_target="tpu_custom_call" | custom-call | flops 6000000000 | bytes 12582912 | tf_op jit(solution)/shard_map/cond/branch_0_fun/transposed_conv/pallas_call | solution.py:358
  144.9 2.6 %all-to-all-done.3.mine_ref = bf16[16,112,128]{2,1,0:T(8,128)(2,1)S(1)} async-done(((bf16[16,112,128]{2,1,0:T(8,128)(2,1)}), bf16[16,112,128]{2,1,0:T(8,128)(2,1)S(1)}, u32[]{:S(2)}, u32[]{:S(2)}) %all-to-all-start.3) | async-done | bytes 458784 | tf_op jit(solution)/shard_map/cond/branch_0_fun/all_to_all | solution.py:663
  147.4 3.8 %collective-permute-start.5 = (bf16[16,112,128]{2,1,0:T(8,128)(2,1)S(1)}, bf16[16,112,128]{2,1,0:T(8,128)(2,1)S(1)}, u32[]{:S(2)}, u32[]{:S(2)}) collective-permute-start(bf16[16,112,128]{2,1,0:T(8,128)(2,1)S(1)} %all-to-all-done.3.mine_ref), channel_id=1, source_target_pairs={{0,1},{1,0},{2,3},{3,2},{4,5},{5,4},{6,7},{7,6},{8,9},{9,8},{10,11... | collective-permute-start | bytes 1376264 | tf_op jit(solution)/shard_map/cond/branch_0_fun/ppermute | solution.py:671
  151.2 1.4 collective-permute-done.5.other_ref
  152.6 0.4 finish.2
  153.2 0.0 copy-start.5
  153.2 1.2 copy-done.5
  (25 shorter events, 0.1 us)
Async XLA Ops:
  0.6 22.8 %copy-start.2 = (bf16[27,128,128]{2,1,0:T(8,128)(2,1)S(1)}, bf16[27,128,128]{2,1,0:T(8,128)(2,1)}, u32[]{:S(2)}) copy-start(bf16[27,128,128]{2,1,0:T(8,128)(2,1)} %w_ref) | copy-start | bytes 2654212
  0.6 10.9 %copy-start.11 = (s32[1,1,2,4]{3,2,1,0:T(2,128)S(1)}, s32[1,1,2,4]{3,2,1,0:T(2,128)}, u32[]{:S(2)}) copy-start(s32[1,1,2,4]{3,2,1,0:T(2,128)} %param.17) | copy-start | bytes 100
  0.7 22.8 %copy-start.14 = (s32[1,1,4,27]{3,2,1,0:T(4,128)S(1)}, s32[1,1,4,27]{3,2,1,0:T(4,128)}, u32[]{:S(2)}) copy-start(s32[1,1,4,27]{3,2,1,0:T(4,128)} %param.15) | copy-start | bytes 1300
  2.8 7.7 %collective-permute-start.16 = (bf16[2,64,128]{2,1,0:T(8,128)(2,1)S(1)}, bf16[2,64,128]{2,1,0:T(8,128)(2,1)S(1)}, u32[]{:S(2)}, u32[]{:S(2)}) collective-permute-start(bf16[2,64,128]{2,1,0:T(8,128)(2,1)S(1)} %get-tuple-element.163), channel_id=1, source_target_pairs={{0,32},{32,64},{64,96},{96,128},{128,160},{160,192},{192,224},{1,3... | collective-permute-start | bytes 98312 | tf_op jit(solution)/shard_map/ppermute | solution.py:174
  6.8 4.7 %collective-permute-start.17 = (bf16[2,64,128]{2,1,0:T(8,128)(2,1)S(1)}, bf16[2,64,128]{2,1,0:T(8,128)(2,1)S(1)}, u32[]{:S(2)}, u32[]{:S(2)}) collective-permute-start(bf16[2,64,128]{2,1,0:T(8,128)(2,1)S(1)} %get-tuple-element.164), channel_id=1, source_target_pairs={{32,0},{64,32},{96,64},{128,96},{160,128},{192,160},{224,192},{33,... | collective-permute-start | bytes 98312 | tf_op jit(solution)/shard_map/ppermute | solution.py:174
  12.3 7.5 %collective-permute-start.18 = (bf16[272,128]{1,0:T(8,128)(2,1)S(1)}, bf16[272,128]{1,0:T(8,128)(2,1)S(1)}, u32[]{:S(2)}, u32[]{:S(2)}) collective-permute-start(bf16[272,128]{1,0:T(8,128)(2,1)S(1)} %get-tuple-element.168), channel_id=1, source_target_pairs={{0,1},{1,2},{2,3},{3,4},{4,5},{5,6},{6,7},{7,8},{8,9},{9,10},{10,1... | collective-permute-start | bytes 208904 | tf_op jit(solution)/shard_map/ppermute | solution.py:174
  17.8 5.6 %collective-permute-start.19 = (bf16[272,128]{1,0:T(8,128)(2,1)S(1)}, bf16[272,128]{1,0:T(8,128)(2,1)S(1)}, u32[]{:S(2)}, u32[]{:S(2)}) collective-permute-start(bf16[272,128]{1,0:T(8,128)(2,1)S(1)} %get-tuple-element.169), channel_id=1, source_target_pairs={{1,0},{2,1},{3,2},{4,3},{5,4},{6,5},{7,6},{8,7},{9,8},{10,9},{11,1... | collective-permute-start | bytes 208904 | tf_op jit(solution)/shard_map/ppermute | solution.py:174
  23.4 39.1 %copy-start.4 = (bf16[1,1,4,512,128]{4,3,2,1,0:T(8,128)(2,1)S(1)}, bf16[1,1,4,512,128]{4,3,2,1,0:T(8,128)(2,1)}, u32[]{:S(2)}) copy-start(bf16[1,1,4,512,128]{4,3,2,1,0:T(8,128)(2,1)} %param.12) | copy-start | bytes 1572868
  23.4 39.1 %copy-start.9 = (s32[1,1,4,512]{3,2,1,0:T(4,128)S(1)}, s32[1,1,4,512]{3,2,1,0:T(4,128)}, u32[]{:S(2)}) copy-start(s32[1,1,4,512]{3,2,1,0:T(4,128)} %param.13) | copy-start | bytes 24580
  23.4 39.1 %copy-start.10 = (s32[1,1,2,2]{3,2,1,0:T(2,128)S(1)}, s32[1,1,2,2]{3,2,1,0:T(2,128)}, u32[]{:S(2)}) copy-start(s32[1,1,2,2]{3,2,1,0:T(2,128)} %param.16) | copy-start | bytes 52
  23.4 39.1 %copy-start.12 = (f32[128]{0:T(128)S(1)}, f32[128]{0:T(128)}, u32[]{:S(2)}) copy-start(f32[128]{0:T(128)} %param.19) | copy-start | bytes 1540
  23.5 39.1 %copy-start.15 = (f32[128]{0:T(128)S(1)}, f32[128]{0:T(128)}, u32[]{:S(2)}) copy-start(f32[128]{0:T(128)} %param.20) | copy-start | bytes 1540
  45.8 15.4 %all-to-all-start.11 = ((f32[16,8,128]{2,1,0:T(8,128)}), f32[16,8,128]{2,1,0:T(8,128)S(1)}, u32[]{:S(2)}, u32[]{:S(2)}) async-start(f32[16,8,128]{2,1,0:T(8,128)} %broadcast_in_dim.29), calls=%async_computation.11 | async-start | bytes 131072 | tf_op jit(solution)/shard_map/all_to_all | solution.py:663
  62.6 9.3 %copy-start.7 = (bf16[4,512,128]{2,1,0:T(8,128)(2,1)}, bf16[4,512,128]{2,1,0:T(8,128)(2,1)S(1)}, u32[]{:S(2)}) copy-start(bf16[4,512,128]{2,1,0:T(8,128)(2,1)S(1)} %get-tuple-element.56.mask_ref) | copy-start | bytes 1572868 | tf_op jit(solution)/shard_map/cond
  71.9 3.8 %collective-permute-start = (bf16[3632,128]{1,0:T(8,128)(2,1)S(1)}, bf16[3632,128]{1,0:T(8,128)(2,1)S(1)}, u32[]{:S(2)}, u32[]{:S(2)}) collective-permute-start(bf16[3632,128]{1,0:T(8,128)(2,1)S(1)} %get-tuple-element.63), channel_id=1, source_target_pairs={{0,1},{1,0},{2,3},{3,2},{4,5},{5,4},{6,7},{7,6},{8,9},{9,8},{10,11... | collective-permute-start | bytes 2789384 | tf_op jit(solution)/shard_map/cond/branch_0_fun/ppermute | solution.py:671
  75.9 31.2 %copy-start.8 = (bf16[4,512,128]{2,1,0:T(8,128)(2,1)S(1)}, bf16[4,512,128]{2,1,0:T(8,128)(2,1)}, u32[]{:S(2)}) copy-start(bf16[4,512,128]{2,1,0:T(8,128)(2,1)} %copy-done.7) | copy-start | bytes 1572868 | tf_op jit(solution)/shard_map/cond
  108.1 30.7 %copy-start.6 = (bf16[3,1152,128]{2,1,0:T(8,128)(2,1)S(1)}, bf16[3,1152,128]{2,1,0:T(8,128)(2,1)}, u32[]{:S(2)}) copy-start(bf16[3,1152,128]{2,1,0:T(8,128)(2,1)} %get-tuple-element.81.w_ref) | copy-start | bytes 2654212 | tf_op jit(solution)/shard_map/cond
  109.3 10.9 %all-to-all-start.2 = ((bf16[8,16,128]{2,1,0:T(8,128)(2,1)}), bf16[8,16,128]{2,1,0:T(8,128)(2,1)S(1)}, u32[]{:S(2)}, u32[]{:S(2)}) async-start(bf16[8,16,128]{2,1,0:T(8,128)(2,1)} %broadcast_in_dim.6), calls=%async_computation.2 | async-start | bytes 65536 | tf_op jit(solution)/shard_map/cond/branch_0_fun/all_to_all | solution.py:663
  112.7 3.1 %collective-permute-start.1 = (bf16[2,64,128]{2,1,0:T(8,128)(2,1)S(1)}, bf16[2,64,128]{2,1,0:T(8,128)(2,1)S(1)}, u32[]{:S(2)}, u32[]{:S(2)}) collective-permute-start(bf16[2,64,128]{2,1,0:T(8,128)(2,1)S(1)} %get-tuple-element.73), channel_id=1, source_target_pairs={{0,32},{32,64},{64,96},{96,128},{128,160},{160,192},{192,224},{1,3... | collective-permute-start | bytes 98312 | tf_op jit(solution)/shard_map/cond/branch_0_fun/ppermute | solution.py:174
  114.5 5.0 %collective-permute-start.2 = (bf16[2,64,128]{2,1,0:T(8,128)(2,1)S(1)}, bf16[2,64,128]{2,1,0:T(8,128)(2,1)S(1)}, u32[]{:S(2)}, u32[]{:S(2)}) collective-permute-start(bf16[2,64,128]{2,1,0:T(8,128)(2,1)S(1)} %get-tuple-element.74), channel_id=1, source_target_pairs={{32,0},{64,32},{96,64},{128,96},{160,128},{192,160},{224,192},{33,... | collective-permute-start | bytes 98312 | tf_op jit(solution)/shard_map/cond/branch_0_fun/ppermute | solution.py:174
  120.2 18.6 %collective-permute-start.3 = (bf16[272,128]{1,0:T(8,128)(2,1)S(1)}, bf16[272,128]{1,0:T(8,128)(2,1)S(1)}, u32[]{:S(2)}, u32[]{:S(2)}) collective-permute-start(bf16[272,128]{1,0:T(8,128)(2,1)S(1)} %get-tuple-element.79), channel_id=1, source_target_pairs={{0,1},{1,2},{2,3},{3,4},{4,5},{5,6},{6,7},{7,8},{8,9},{9,10},{10,1... | collective-permute-start | bytes 208904 | tf_op jit(solution)/shard_map/cond/branch_0_fun/ppermute | solution.py:174
  127.7 11.1 %collective-permute-start.4 = (bf16[272,128]{1,0:T(8,128)(2,1)S(1)}, bf16[272,128]{1,0:T(8,128)(2,1)S(1)}, u32[]{:S(2)}, u32[]{:S(2)}) collective-permute-start(bf16[272,128]{1,0:T(8,128)(2,1)S(1)} %get-tuple-element.80), channel_id=1, source_target_pairs={{1,0},{2,1},{3,2},{4,3},{5,4},{6,5},{7,6},{8,7},{9,8},{10,9},{11,1... | collective-permute-start | bytes 208904 | tf_op jit(solution)/shard_map/cond/branch_0_fun/ppermute | solution.py:174
  130.5 16.9 %all-to-all-start.3 = ((bf16[16,112,128]{2,1,0:T(8,128)(2,1)}), bf16[16,112,128]{2,1,0:T(8,128)(2,1)S(1)}, u32[]{:S(2)}, u32[]{:S(2)}) async-start(bf16[16,112,128]{2,1,0:T(8,128)(2,1)} %broadcast_in_dim.7), calls=%async_computation.3 | async-start | bytes 917504 | tf_op jit(solution)/shard_map/cond/branch_0_fun/all_to_all | solution.py:663
  147.4 5.2 %collective-permute-start.5 = (bf16[16,112,128]{2,1,0:T(8,128)(2,1)S(1)}, bf16[16,112,128]{2,1,0:T(8,128)(2,1)S(1)}, u32[]{:S(2)}, u32[]{:S(2)}) collective-permute-start(bf16[16,112,128]{2,1,0:T(8,128)(2,1)S(1)} %all-to-all-done.3.mine_ref), channel_id=1, source_target_pairs={{0,1},{1,0},{2,3},{3,2},{4,5},{5,4},{6,7},{7,6},{8,9},{9,8},{10,11... | collective-permute-start | bytes 1376264 | tf_op jit(solution)/shard_map/cond/branch_0_fun/ppermute | solution.py:671
  153.2 1.2 copy-start.5
where the time goes:
time: 155 us; the launch traced here: 154 us
  starting transfers between devices  51.3 us (33%)
  blocking collectives  47 us (30%)
  Pallas kernels  28.5 us (18%)
  waiting for transfers between devices  21 us (14%)
  local copies, waits for them, and re-layouts  3.37 us (2%)
  between operations  2.21 us (1%)
    ppermute x8, starting transfers between devices, neighbours(): return (lax.ppermute(high, axis, up), lax.ppermute(low, axis, down))  25.3 us
    all_to_all x3, starting transfers between devices, spread(): lax.all_to_all(jnp.broadcast_to(value[None], (size,) + value.shape), axes...  20.6 us
    all_to_all x1, blocking collectives, second(): parts = lax.all_to_all(join(keep, swap(send)), CROSS, 0, 0)  20.2 us
    all_to_all x1, blocking collectives, spread(): lax.all_to_all(jnp.broadcast_to(value[None], (size,) + value.shape), axes...  16 us
    all_to_all x1, blocking collectives, second(): parts = lax.all_to_all(middle(parts), 'z', 0, 0)  10.8 us
    pallas_call x1, Pallas kernels, wgrad(): pl.pallas_call(functools.partial(wgrad_kernel, unroll=unroll), out_shape=...  9.25 us
    all_to_all x3, waiting for transfers between devices, spread(): lax.all_to_all(jnp.broadcast_to(value[None], (size,) + value.shape), axes...  9.08 us
    ppermute x8, waiting for transfers between devices, neighbours(): return (lax.ppermute(high, axis, up), lax.ppermute(low, axis, down))  8.31 us
  transfers between devices with their start and end apart: 13, of which 7 were waited for; matrix products, arithmetic and copies ran while one was open for 1% of the time, Pallas kernels for 6%

commit v1 on v0

--- a/solution.py
+++ b/solution.py
@@ -39,12 +39,24 @@
     return jax.ShapeDtypeStruct(dims, kind)
 
 
-def pick_x(sends_ref, own_ref, low_ref, high_ref, faces):
-    for side, out_ref in ((0, low_ref), (1, high_ref)):
-        start, stop = (0, VOX) if not faces else ((0, PLANE), (VOX - PLANE, VOX))[side]
+def side_of(turn, odd):
+    return odd if turn else 1 - odd
+
+
+def lower_upper(odd, first, second):
+    even = odd == 0
+    return jnp.where(even, second, first), jnp.where(even, first, second)
+
+
+def pick_x(place_ref, sends_ref, own_ref, first_ref, second_ref, faces):
+    for turn, out_ref in ((0, first_ref), (1, second_ref)):
+        side, rows = turn, slice(0, VOX)
+        if faces:
+            side = side_of(turn, place_ref[0])
+            rows = pl.ds(pl.multiple_of(side * (VOX - PLANE), PLANE), PLANE)
         for k in range(HX):
             row = sends_ref[side, k]
-            brick = own_ref[jnp.minimum(row, SLOTS - 1), start:stop, :]
+            brick = own_ref[jnp.minimum(row, SLOTS - 1), rows, :]
             out_ref[k] = jnp.where(row < SLOTS, brick, jnp.zeros_like(brick))
 
 
@@ -54,7 +66,7 @@
 
 
 def prepare_kernel(
-    counts_ref, sends_ref, feat_ref, occ_ref, own_ref, mask_ref, low_ref, high_ref, *, faces
+    place_ref, counts_ref, sends_ref, feat_ref, occ_ref, own_ref, mask_ref, low_ref, high_ref, *, faces
 ):
     for s in range(SLOTS):
         live = (s < counts_ref[0, 0]).astype(F32)
@@ -64,22 +76,22 @@
             rows = pl.ds(k * CH, CH)
             mask_ref[s, rows, :] = column.astype(BF16)
             own_ref[s, rows, :] = (feat_ref[s, rows, :].astype(F32) * column).astype(BF16)
-    pick_x(sends_ref, own_ref, low_ref, high_ref, faces)
-
-
-def prepare(counts, sends_x, features, occupancy, faces):
+    pick_x(place_ref, sends_ref, own_ref, low_ref, high_ref, faces)
+
+
+def prepare(place, counts, sends_x, features, occupancy, faces):
     return pl.pallas_call(
         functools.partial(prepare_kernel, faces=faces),
         out_shape=(shape((SLOTS, VOX, CH), BF16),) * 2 + x_shapes(faces),
-        in_specs=[SM, SM, VM, VM],
+        in_specs=[SM, SM, SM, VM, VM],
         out_specs=(VM, VM, VM, VM),
         compiler_params=params(),
         cost_estimate=cost(1 << 20, 2 << 20),
         name="prepare",
-    )(counts, sends_x, features, occupancy)
-
-
-def pick_y_kernel(sends_ref, own_ref, xl_ref, xu_ref, low_ref, high_ref):
+    )(place, counts, sends_x, features, occupancy)
+
+
+def pick_y_kernel(place_ref, sends_ref, own_ref, xl_ref, xu_ref, low_ref, high_ref):
     for side, out_ref in ((0, low_ref), (1, high_ref)):
         for k in range(HY):
             row = sends_ref[side, k]
@@ -101,14 +113,19 @@
                 out_ref[k] = jnp.zeros((VOX, CH), BF16)
 
 
-def pick_y_faces_kernel(sends_ref, own_ref, xl_ref, xu_ref, low_ref, high_ref):
+def pick_y_faces_kernel(place_ref, sends_ref, own_ref, x1_ref, x2_ref, first_ref, second_ref):
     lines = lax.broadcasted_iota(jnp.int32, (16, CH), 0)
-    for side, out_ref in ((0, low_ref), (1, high_ref)):
-        skip = 0 if side == 0 else PLANE - 16
+    odd = place_ref[0]
+    for turn, out_ref in ((0, first_ref), (1, second_ref)):
+        side = side_of(turn, place_ref[1])
+        skip = side * (PLANE - 16)
+
+        def piece(base):
+            return pl.ds(pl.multiple_of(base + skip, 16), 16)
 
         def edge(block):
             block = block.astype(F32)
-            return block[:EDGE] if side == 0 else block[EDGE:]
+            return jnp.where(side == 0, block[:EDGE], block[EDGE:])
 
         origin = jnp.zeros((16, CH), F32)
         for k in range(HY):
@@ -122,23 +139,19 @@
             @pl.when(row < SLOTS)
             def _():
                 brick = jnp.minimum(row, SLOTS - 1)
-                parts = [
-                    edge(own_ref[brick, a * PLANE + skip : a * PLANE + skip + 16, :])
-                    for a in range(EDGE)
-                ]
+                parts = [edge(own_ref[brick, piece(a * PLANE), :]) for a in range(EDGE)]
                 out_ref[rows, :] = jnp.concatenate(parts, axis=0).astype(BF16)
 
-            @pl.when(lower)
+            @pl.when(lower | upper)
             def _():
-                part = edge(xl_ref[jnp.clip(row - SLOTS, 0, HX - 1), skip : skip + 16, :])
-                empty = jnp.zeros((PLANE - EDGE, CH), F32)
-                out_ref[rows, :] = jnp.concatenate((empty, part), axis=0).astype(BF16)
-
-            @pl.when(upper)
-            def _():
-                part = edge(xu_ref[jnp.clip(row - SLOTS - HX, 0, HX - 1), skip : skip + 16, :])
-                empty = jnp.zeros((PLANE - EDGE, CH), F32)
-                out_ref[rows, :] = jnp.concatenate((part, empty), axis=0).astype(BF16)
+                at = jnp.where(lower, row - SLOTS, row - SLOTS - HX)
+                at = jnp.clip(at, 0, HX - 1)
+                down, up = lower_upper(odd, x1_ref[at, piece(0), :], x2_ref[at, piece(0), :])
+                part = edge(jnp.where(lower, down, up))
+                empty = jnp.zeros((PLANE - 2 * EDGE, CH), F32)
+                blank = jnp.zeros_like(part)
+                front, back = jnp.where(lower, blank, part), jnp.where(lower, part, blank)
+                out_ref[rows, :] = jnp.concatenate((front, empty, back), axis=0).astype(BF16)
 
             @pl.when(row >= SLOTS + 2 * HX)
             def _():
@@ -147,17 +160,17 @@
         out_ref[HY * PLANE : FACE_ROWS, :] = origin.astype(BF16)
 
 
-def pick_y(sends_y, own, xl, xu, faces):
+def pick_y(place, sends_y, own, xl, xu, faces):
     send = shape((FACE_ROWS, CH) if faces else (HY, VOX, CH), BF16)
     return pl.pallas_call(
         pick_y_faces_kernel if faces else pick_y_kernel,
         out_shape=(send, send),
-        in_specs=[SM, VM, VM, VM],
+        in_specs=[SM, SM, VM, VM, VM],
         out_specs=(VM, VM),
         compiler_params=params(),
         cost_estimate=cost(1 << 20, 2 << 20),
         name="pick_y",
-    )(sends_y, own, xl, xu)
+    )(place, sends_y, own, xl, xu)
 
 
 def axis_size(axes):
@@ -167,53 +180,75 @@
     return size
 
 
-def neighbours(low, high, axis):
-    size = axis_size(axis)
+def neighbours(first, second, axes, faces):
+    size = axis_size(axes)
+    if faces:
+        pairs = [[(i, i + 1) for i in range(turn, size - 1, 2)] for turn in (0, 1)]
+        one, two = [pair + [(j, i) for i, j in pair] for pair in pairs]
+        return lax.ppermute(first, axes, one), lax.ppermute(second, axes, two)
     up = [(i, i + 1) for i in range(size - 1)]
     down = [(j, i) for i, j in up]
-    return lax.ppermute(high, axis, up), lax.ppermute(low, axis, down)
-
-
-def fill_columns(map_ref, slot, table_ref, x9_ref):
+    return lax.ppermute(second, axes, up), lax.ppermute(first, axes, down)
+
+
+def fill_plane(map_ref, slot, table_ref, x9_ref, move, base, row):
     sub = lax.broadcasted_iota(jnp.int32, (EDGE + 2, EDGE, CH), 1)
-    for a in range(-1, EDGE + 1):
-        move = -1 if a < 0 else (1 if a >= EDGE else 0)
-        base = (a % EDGE) * PLANE
-        spans = []
-        for r in (-1, 0, 1):
-            tap = 9 * (move + 1) + r + 1
-            before = table_ref[map_ref[slot, tap], base + 48 : base + 64, :].astype(F32)[8:]
-            middle = table_ref[map_ref[slot, tap + 3], base : base + 64, :].astype(F32)
-            after = table_ref[map_ref[slot, tap + 6], base : base + 16, :].astype(F32)[:8]
-            spans.append(jnp.concatenate((before, middle, after), axis=0).reshape(EDGE + 2, EDGE, CH))
-        low, centre, high = spans
-        down = pltpu.roll(jnp.where(sub == EDGE - 1, low, centre), 1, 1)
-        up = pltpu.roll(jnp.where(sub == 0, high, centre), EDGE - 1, 1)
-        for r, source in ((-1, down), (0, centre), (1, up)):
-            for q in (-1, 0, 1):
-                rows = source[q + 1 : q + 1 + EDGE].reshape(PLANE, CH).astype(BF16)
-                lane = (3 * (q + 1) + r + 1) * CH
-                x9_ref[(a + 1) * PLANE : (a + 2) * PLANE, lane : lane + CH] = rows
-
-
-def fill_whole(table_ref, refs):
+    spans = []
+    for r in (-1, 0, 1):
+        tap = 9 * (move + 1) + r + 1
+        first, whole_plane, last = pl.ds(base + 48, 16), pl.ds(base, PLANE), pl.ds(base, 16)
+        before = table_ref[map_ref[slot, tap], first, :].astype(F32)[8:]
+        middle = table_ref[map_ref[slot, tap + 3], whole_plane, :].astype(F32)
+        after = table_ref[map_ref[slot, tap + 6], last, :].astype(F32)[:8]
+        spans.append(jnp.concatenate((before, middle, after), axis=0).reshape(EDGE + 2, EDGE, CH))
+    low, centre, high = spans
+    down = pltpu.roll(jnp.where(sub == EDGE - 1, low, centre), 1, 1)
+    up = pltpu.roll(jnp.where(sub == 0, high, centre), EDGE - 1, 1)
+    for r, source in ((-1, down), (0, centre), (1, up)):
+        for q in (-1, 0, 1):
+            rows = source[q + 1 : q + 1 + EDGE].reshape(PLANE, CH).astype(BF16)
+            lane = (3 * (q + 1) + r + 1) * CH
+            x9_ref[pl.ds(row, PLANE), lane : lane + CH] = rows
+
+
+def fill_columns(map_ref, slot, table_ref, x9_ref, unroll=True):
+    fill = functools.partial(fill_plane, map_ref, slot, table_ref, x9_ref)
+    fill(-1, VOX - PLANE, 0)
+    if unroll:
+        for a in range(EDGE):
+            fill(0, a * PLANE, (a + 1) * PLANE)
+    else:
+
+        def inner(a, carry):
+            base = pl.multiple_of(a * PLANE, PLANE)
+            fill(0, base, pl.multiple_of(base + PLANE, PLANE))
+            return carry
+
+        lax.fori_loop(0, EDGE, inner, 0)
+    fill(1, 0, (EDGE + 1) * PLANE)
+
+
+def fill_whole(place_ref, table_ref, refs):
     start = 0
     for ref in refs:
         table_ref[start : start + ref.shape[0]] = ref[...]
         start += ref.shape[0]
 
 
-def fill_faces(table_ref, refs):
-    own_ref, xl_ref, xu_ref, yl_ref, yu_ref = refs
+def fill_faces(place_ref, table_ref, refs):
+    own_ref, x1_ref, x2_ref, y1_ref, y2_ref = refs
     table_ref[0:SLOTS] = own_ref[...]
     for k in range(HX):
-        table_ref[SLOTS + k, VOX - PLANE : VOX, :] = xl_ref[k]
-        table_ref[SLOTS + HX + k, 0:PLANE, :] = xu_ref[k]
+        low, high = lower_upper(place_ref[0], x1_ref[k], x2_ref[k])
+        table_ref[SLOTS + k, VOX - PLANE : VOX, :] = low
+        table_ref[SLOTS + HX + k, 0:PLANE, :] = high
     empty = jnp.zeros((EDGE, CH), F32)
     first = SLOTS + 2 * HX
     for k in range(HY):
-        low = yl_ref[k * PLANE : (k + 1) * PLANE, :].astype(F32)
-        high = yu_ref[k * PLANE : (k + 1) * PLANE, :].astype(F32)
+        rows = slice(k * PLANE, (k + 1) * PLANE)
+        low, high = lower_upper(
+            place_ref[1], y1_ref[rows, :].astype(F32), y2_ref[rows, :].astype(F32)
+        )
         for a in range(EDGE):
             part = slice(a * EDGE, (a + 1) * EDGE)
             base = a * PLANE
@@ -225,17 +260,20 @@
             ).astype(BF16)
 
 
-def count_misfits(rows, yl_ref, yu_ref):
+def count_misfits(place_ref, rows, y1_ref, y2_ref):
     lane = lax.broadcasted_iota(jnp.int32, rows.shape, 1)
     within = lane - jnp.where(lane >= 9, 9, 0) - jnp.where(lane >= 18, 9, 0)
     not_down, not_up = lane >= 9, lane < 18
     bad = (rows >= SLOTS) & (rows < SLOTS + HX) & not_down
     bad = bad | ((rows >= SLOTS + HX) & (rows < SLOTS + 2 * HX) & not_up)
-    for start, ref, wrong in (
-        (SLOTS + 2 * HX, yl_ref, within >= 3),
-        (SLOTS + 2 * HX + HY, yu_ref, within < 6),
+    marks = slice(HY * PLANE, FACE_ROWS)
+    low, high = lower_upper(
+        place_ref[1], y1_ref[marks, :].astype(F32), y2_ref[marks, :].astype(F32)
+    )
+    for start, origin, wrong in (
+        (SLOTS + 2 * HX, low, within >= 3),
+        (SLOTS + 2 * HX + HY, high, within < 6),
     ):
-        origin = ref[HY * PLANE : FACE_ROWS, :].astype(F32)
         for k in range(HY):
             code = jnp.broadcast_to(origin[k : k + 1, 0 : rows.shape[1]], rows.shape)
             fault = wrong | ((code == 1.0) & not_down) | ((code == 2.0) & not_up)
@@ -244,10 +282,10 @@
 
 
 def conv_kernel(
-    map_ref, rows_ref, own_ref, xl_ref, xu_ref, yl_ref, yu_ref, w_ref, mask_ref,
+    place_ref, map_ref, rows_ref, own_ref, xl_ref, xu_ref, yl_ref, yu_ref, w_ref, mask_ref,
     out_ref, x9_out, stat_ref, table_ref, x9_ref, sems,
 ):
-    fill_faces(table_ref, (own_ref, xl_ref, xu_ref, yl_ref, yu_ref))
+    fill_faces(place_ref, table_ref, (own_ref, xl_ref, xu_ref, yl_ref, yu_ref))
     table_ref[16] = jnp.zeros((VOX, CH), BF16)
     sums = [jnp.zeros((1, CH), F32)] * 3
     copies = []
@@ -272,19 +310,19 @@
         out_ref[slot] = total
         terms = (masked, masked * total, mask)
         sums = [s + jnp.sum(term, axis=0, keepdims=True) for s, term in zip(sums, terms)]
-    misfits = count_misfits(rows_ref[...], yl_ref, yu_ref)
+    misfits = count_misfits(place_ref, rows_ref[...], yl_ref, yu_ref)
     sums.append(jnp.broadcast_to(misfits, (1, CH)))
     stat_ref[...] = jnp.concatenate(sums + [jnp.zeros((4, CH), F32)], axis=0)
     for copy in copies:
         copy.wait()
 
 
-def conv(row_map, own, xl, xu, yl, yu, weight, mask):
+def conv(place, row_map, own, xl, xu, yl, yu, weight, mask):
     columns = (SLOTS, 10 * PLANE, 9 * CH)
     return pl.pallas_call(
         conv_kernel,
         out_shape=(shape((SLOTS, VOX, CH), F32), shape(columns, BF16), shape((8, CH), F32)),
-        in_specs=[SM] + [VM] * 8,
+        in_specs=[SM, SM] + [VM] * 8,
         out_specs=(VM, pl.BlockSpec(memory_space=pl.ANY), VM),
         scratch_shapes=[
             pltpu.VMEM((17, VOX, CH), BF16),
@@ -294,11 +332,12 @@
         compiler_params=params(28),
         cost_estimate=cost(6000000000, 12 << 20),
         name="forward_conv",
-    )(row_map, row_map, own, xl, xu, yl, yu, weight, mask)
+    )(place, row_map, row_map, own, xl, xu, yl, yu, weight, mask)
 
 
 def step_kernel(
-    map_ref, rows_ref, own_ref, xl_ref, xu_ref, yl_ref, yu_ref, w_ref, mask_ref, *rest, forward, faces
+    place_ref, map_ref, rows_ref, own_ref, xl_ref, xu_ref, yl_ref, yu_ref, w_ref, mask_ref, *rest,
+    forward, faces
 ):
     slot = pl.program_id(0)
     if forward:
@@ -310,16 +349,12 @@
     @pl.when(slot == 0)
     def _():
         fill = fill_faces if faces else fill_whole
-        fill(table_ref, (own_ref, xl_ref, xu_ref, yl_ref, yu_ref))
+        fill(place_ref, table_ref, (own_ref, xl_ref, xu_ref, yl_ref, yu_ref))
         table_ref[16] = jnp.zeros((VOX, CH), BF16)
         if forward:
             stat_ref[...] = jnp.zeros_like(stat_ref)
-            if faces:
-                stat_ref[3:4] = jnp.broadcast_to(
-                    count_misfits(rows_ref[...], yl_ref, yu_ref), (1, CH)
-                )
-
-    fill_columns(map_ref, slot, table_ref, x9_ref)
+
+    fill_columns(map_ref, slot, table_ref, x9_ref, faces)
     total = None
     for p in range(3):
         term = jnp.dot(
@@ -341,7 +376,7 @@
     return pl.BlockSpec(dims, lambda s: (0,) * len(dims))
 
 
-def conv_steps(row_map, own, xl, xu, yl, yu, weight, mask, forward, faces):
+def conv_steps(place, row_map, own, xl, xu, yl, yu, weight, mask, forward, faces):
     brick = pl.BlockSpec((1, VOX, CH), lambda s: (s, 0, 0))
     scratch = [pltpu.VMEM((17, VOX, CH), BF16)]
     if forward:
@@ -360,6 +395,7 @@
         grid=(SLOTS,),
         out_shape=out_shape,
         in_specs=[
+            SM,
             SM,
             whole(*row_map.shape),
             whole(*own.shape),
@@ -375,7 +411,7 @@
         compiler_params=params(24),
         cost_estimate=cost(6000000000, 12 << 20),
         name="forward_steps" if forward else "transposed_conv",
-    )(row_map, row_map, own, xl, xu, yl, yu, weight, mask)
+    )(place, row_map, row_map, own, xl, xu, yl, yu, weight, mask)
 
 
 def norm_terms(stats):
@@ -431,7 +467,7 @@
 
 
 def wgrad_kernel(
-    core_ref, stat_ref, conv_ref, cot_ref, mask_ref, gain_ref, shift_ref, x9_hbm,
+    place_ref, stat_ref, conv_ref, cot_ref, mask_ref, gain_ref, shift_ref, x9_hbm,
     act_ref, ga_ref, norm_ref, keep_ref, send_ref, g_ref, x9_ref, hold_ref, sems, *, unroll
 ):
     copies = [
@@ -486,12 +522,12 @@
     for half in (0, 1):
         rows = jnp.concatenate(ones[13 * half : 13 * half + 14], axis=0)
         hold_ref[half, 16 * MAIN : 16 * MAIN + EXTRA, :] = pack(rows, sums).astype(F32)
-    core = core_ref[0]
+    core = place_ref[1]
     keep_ref[...] = hold_ref[core]
     send_ref[...] = hold_ref[1 - core].astype(BF16)
 
 
-def wgrad(core, stats, conv_out, cotangent, mask, gain, shift, x9, unroll):
+def wgrad(place, stats, conv_out, cotangent, mask, gain, shift, x9, unroll):
     rows = 16 * MAIN + EXTRA
     return pl.pallas_call(
         functools.partial(wgrad_kernel, unroll=unroll),
@@ -513,7 +549,7 @@
         compiler_params=params(28),
         cost_estimate=cost(6000000000, 12 << 20),
         name="weight_terms",
-    )(core, stats, conv_out, cotangent, mask, gain, shift, x9)
+    )(place, stats, conv_out, cotangent, mask, gain, shift, x9)
 
 
 def join_kernel(keep_ref, got_ref, out_ref):
@@ -573,7 +609,7 @@
     return jnp.transpose(jnp.broadcast_to(row, (CH, CH)))
 
 
-def combine_kernel(block_ref, parts_ref, norm_ref, gain_ref, out_ref, gg_ref, sg_ref, coef_ref):
+def combine_kernel(place_ref, parts_ref, norm_ref, gain_ref, out_ref, gg_ref, sg_ref, coef_ref):
     total = jnp.sum(parts_ref[...], axis=0)
     main, ones, sums = total[0:32], total[32:34], total[34:36]
     inverse, count = norm_ref[1:2], norm_ref[2:3]
@@ -583,30 +619,32 @@
     coef_ref[0] = column(gain_ref[...] * inverse * scale)
     coef_ref[1] = column(sums[0:1] / count)
     coef_ref[2] = column(sums[1:2] / count)
-    mine = pl.ds(pl.multiple_of(block_ref[0] * 8, 8), 8)
+    mine = pl.ds(pl.multiple_of(place_ref[2] * 8, 8), 8)
     factor, first, second = coef_ref[0, mine, :], coef_ref[1, mine, :], coef_ref[2, mine, :]
     values = []
     for i in range(2):
         base, cross = main[16 * i : 16 * i + 8], main[16 * i + 8 : 16 * i + 16]
         values.append(factor * (base - first * ones[i : i + 1] - second * cross))
-    out_ref[...] = jnp.concatenate(values, axis=0).astype(BF16)
-
-
-def combine(block, parts, norm, gain):
+    value = jnp.concatenate(values, axis=0).astype(BF16)
+    for z in range(8):
+        out_ref[z] = value
+
+
+def combine(place, parts, norm, gain):
     return pl.pallas_call(
         combine_kernel,
-        out_shape=(shape((16, CH), BF16), shape((1, CH), F32), shape((1, CH), F32)),
+        out_shape=(shape((8, 16, CH), BF16), shape((1, CH), F32), shape((1, CH), F32)),
         in_specs=[SM] + [VM] * 3,
         out_specs=(VM,) * 3,
         scratch_shapes=[pltpu.VMEM((3, CH, CH), F32)],
         compiler_params=params(),
         cost_estimate=cost(1 << 20, 1 << 20),
         name="combine",
-    )(block, parts, norm, gain)
+    )(place, parts, norm, gain)
 
 
 def grad_kernel(
-    sends_ref, parts_ref, norm_ref, gain_ref, conv_ref, ga_ref, mask_ref, out_ref, low_ref, high_ref, *, faces
+    place_ref, sends_ref, parts_ref, norm_ref, gain_ref, conv_ref, ga_ref, mask_ref, out_ref, low_ref, high_ref, *, faces
 ):
     totals = jnp.sum(parts_ref[...], axis=0)[34:36]
     mean, inverse, count = norm_ref[0:1], norm_ref[1:2], norm_ref[2:3]
@@ -615,24 +653,24 @@
         normed = (conv_ref[s] - mean) * inverse
         inner = ga_ref[s] - (totals[0:1] + normed * totals[1:2]) / count
         out_ref[s] = (factor * inner * mask_ref[s].astype(F32)).astype(BF16)
-    pick_x(sends_ref, out_ref, low_ref, high_ref, faces)
-
-
-def grad(sends_x, parts, norm, gain, conv_out, ga, mask, faces):
+    pick_x(place_ref, sends_ref, out_ref, low_ref, high_ref, faces)
+
+
+def grad(place, sends_x, parts, norm, gain, conv_out, ga, mask, faces):
     return pl.pallas_call(
         functools.partial(grad_kernel, faces=faces),
         out_shape=(shape((SLOTS, VOX, CH), BF16),) + x_shapes(faces),
-        in_specs=[SM] + [VM] * 6,
+        in_specs=[SM, SM] + [VM] * 6,
         out_specs=(VM,) * 3,
         compiler_params=params(),
         cost_estimate=cost(4 << 20, 4 << 20),
         name="grad_conv",
-    )(sends_x, parts, norm, gain, conv_out, ga, mask)
-
-
-def finish_kernel(core_ref, mine_ref, other_ref, out_ref):
+    )(place, sends_x, parts, norm, gain, conv_out, ga, mask)
+
+
+def finish_kernel(place_ref, mine_ref, other_ref, out_ref):
     for half in (0, 1):
-        here = core_ref[0] == half
+        here = place_ref[1] == half
         for z in range(7):
             pairs = []
             for k in range(16):
@@ -646,7 +684,7 @@
                 out_ref[tap] = jnp.transpose(rows)
 
 
-def finish(core, mine, other):
+def finish(place, mine, other):
     return pl.pallas_call(
         finish_kernel,
         out_shape=shape((27, CH, CH), F32),
@@ -655,7 +693,7 @@
         compiler_params=params(),
         cost_estimate=cost(1 << 20, 3 << 20),
         name="finish",
-    )(core, mine, other)
+    )(place, mine, other)
 
 
 def spread(value, axes):
@@ -703,39 +741,38 @@
 ):
     row_map, sends_x, sends_y = kernel_map[0, 0], x_send[0, 0], y_send[0, 0]
     gain, shift = norm_gain.reshape(1, CH), norm_shift.reshape(1, CH)
-    core = lax.axis_index("c").reshape(1)
-    block = lax.axis_index(CROSS).reshape(1)
+    place = jnp.stack((lax.axis_index("y") % 2, lax.axis_index("c"), lax.axis_index(CROSS)))
     ahead = weight.reshape(3, 9 * CH, CH)
 
     def first(faces):
-        own, mask, low, high = prepare(counts, sends_x, features[0, 0], occupancy[0, 0], faces)
+        own, mask, low, high = prepare(place, counts, sends_x, features[0, 0], occupancy[0, 0], faces)
         later, low, high = lax.optimization_barrier((weight, low, high))
-        xl, xu = neighbours(low, high, ("xh", "y"))
+        xl, xu = neighbours(low, high, ("xh", "y"), faces)
         xl, xu, turned = lax.optimization_barrier((xl, xu, turn(later)))
-        low, high = pick_y(sends_y, own, xl, xu, faces)
-        yl, yu = neighbours(low, high, ("xl", "z", "c"))
-        table = (row_map, own, xl, xu, yl, yu, ahead, mask)
+        low, high = pick_y(place, sends_y, own, xl, xu, faces)
+        yl, yu = neighbours(low, high, ("xl", "z", "c"), faces)
+        table = (place, row_map, own, xl, xu, yl, yu, ahead, mask)
         conv_out, x9, stats = conv(*table) if faces else conv_steps(*table, True, False)
         return conv_out, x9, mask, turned, all_sum_parts(stats)
 
     def second(conv_out, x9, mask, turned, stats, faces):
         activations, ga, norm, keep, send = wgrad(
-            core, stats, conv_out, cotangent[0, 0], mask, gain, shift, x9, faces
+            place, stats, conv_out, cotangent[0, 0], mask, gain, shift, x9, faces
         )
         parts = lax.all_to_all(join(keep, swap(send)), CROSS, 0, 0)
         parts = lax.all_to_all(middle(parts), "z", 0, 0)
-        grads, low, high = grad(sends_x, parts, norm, gain, conv_out, ga, mask, faces)
+        grads, low, high = grad(place, sends_x, parts, norm, gain, conv_out, ga, mask, faces)
         parts, low, high = lax.optimization_barrier((parts, low, high))
-        xl, xu = neighbours(low, high, ("xh", "y"))
-        value, gain_grad, shift_grad = combine(block, parts, norm, gain)
-        mine = spread(value, ("z",)).reshape(8 * 16, CH)[: 7 * 16]
-        low, high = pick_y(sends_y, grads, xl, xu, faces)
+        xl, xu = neighbours(low, high, ("xh", "y"), faces)
+        value, gain_grad, shift_grad = combine(place, parts, norm, gain)
+        mine = lax.all_to_all(value, "z", 0, 0).reshape(8 * 16, CH)[: 7 * 16]
+        low, high = pick_y(place, sends_y, grads, xl, xu, faces)
         mine, low, high = lax.optimization_barrier((mine, low, high))
-        yl, yu = neighbours(low, high, ("xl", "z", "c"))
+        yl, yu = neighbours(low, high, ("xl", "z", "c"), faces)
         mine = spread(mine, CROSS)
-        features_grad = conv_steps(row_map, grads, xl, xu, yl, yu, turned, mask, False, faces)
+        features_grad = conv_steps(place, row_map, grads, xl, xu, yl, yu, turned, mask, False, faces)
         mine, features_grad = lax.optimization_barrier((mine, features_grad))
-        weight_grad = finish(core, mine, swap(mine))
+        weight_grad = finish(place, mine, swap(mine))
         return activations, features_grad, weight_grad, gain_grad, shift_grad
 
     state = first(True)

time: 155 us -> 145 us (0.935)
  starting transfers between devices: 51.3 us -> 40.1 us
    ppermute x8, starting transfers between devices: 25.3 us -> 14 us  [neighbours(): return (lax.ppermute(first, axes, one), lax.ppermute(second, axes, two))]
    all_to_all x3 -> x2, starting transfers between devices: 20.6 us -> 17.2 us  [spread(): lax.all_to_all(jnp.broadcast_to(value[None], (size,) + value.shape), axes...]
    all_to_all x0 -> x1, starting transfers between devices: none -> 3.34 us  [second(): mine = lax.all_to_all(value, 'z', 0, 0).reshape(8 * 16, CH)[:7 * 16]]
    all_to_all x0 -> x1, waiting for transfers between devices: none -> 3.2 us  [second(): mine = lax.all_to_all(value, 'z', 0, 0).reshape(8 * 16, CH)[:7 * 16]]
    ppermute x8, waiting for transfers between devices: 8.31 us -> 5.19 us  [neighbours(): return (lax.ppermute(first, axes, one), lax.ppermute(second, axes, two))]
    all_to_all x3 -> x2, waiting for transfers between devices: 9.08 us -> 9.06 us  [spread(): lax.all_to_all(jnp.broadcast_to(value[None], (size,) + value.shape), axes...]
where the time goes in v1:
time: 145 us; the launch traced here: 144 us
  blocking collectives  47.4 us (33%)
  starting transfers between devices  40.1 us (28%)
  Pallas kernels  29.8 us (21%)
  waiting for transfers between devices  21 us (14%)
  local copies, waits for them, and re-layouts  2.75 us (2%)
  between operations  2.2 us (2%)
    all_to_all x1, blocking collectives, second(): parts = lax.all_to_all(join(keep, swap(send)), CROSS, 0, 0)  20.2 us
    all_to_all x2, starting transfers between devices, spread(): lax.all_to_all(jnp.broadcast_to(value[None], (size,) + value.shape), axes...  17.2 us
    all_to_all x1, blocking collectives, spread(): lax.all_to_all(jnp.broadcast_to(value[None], (size,) + value.shape), axes...  16.4 us
    ppermute x8, starting transfers between devices, neighbours(): return (lax.ppermute(first, axes, one), lax.ppermute(second, axes, two))  14 us
    all_to_all x1, blocking collectives, second(): parts = lax.all_to_all(middle(parts), 'z', 0, 0)  10.8 us
    pallas_call x1, Pallas kernels, wgrad(): pl.pallas_call(functools.partial(wgrad_kernel, unroll=unroll), out_shape=...  9.14 us
    all_to_all x2, waiting for transfers between devices, spread(): lax.all_to_all(jnp.broadcast_to(value[None], (size,) + value.shape), axes...  9.06 us
    pallas_call x1, Pallas kernels, conv_steps(): pl.pallas_call(functools.partial(step_kernel, forward=forward, faces=face...  6.01 us
  transfers between devices with their start and end apart: 13, of which 7 were waited for; matrix products, arithmetic and copies ran while one was open for 1% of the time, Pallas kernels for 6%

profile of v1, /device:TPU:1, one launch (start us, length us, event | category | flops | bytes accessed | tf_op | source)
XLA Modules:
  0.0 144.4 jit_solution(5172959020994586704)
XLA Ops:
  0.6 0.0 copy-start.2
  1.4 0.1 pad_add_fusion.place_ref
  1.5 1.4 prepare.3
  2.9 2.2 %collective-permute-start.16 = (bf16[2,64,128]{2,1,0:T(8,128)(2,1)S(1)}, bf16[2,64,128]{2,1,0:T(8,128)(2,1)S(1)}, u32[]{:S(2)}, u32[]{:S(2)}) collective-permute-start(bf16[2,64,128]{2,1,0:T(8,128)(2,1)S(1)} %get-tuple-element.157), channel_id=1, source_target_pairs={{0,32},{64,96},{128,160},{192,224},{32,0},{96,64},{160,128},{224,1... | collective-permute-start | bytes 98312 | tf_op jit(solution)/shard_map/ppermute | solution.py:188
  5.1 0.7 collective-permute-start.17
  5.8 2.5 %turn.3 = bf16[3,1152,128]{2,1,0:T(8,128)(2,1)} custom-call(bf16[27,128,128]{2,1,0:T(8,128)(2,1)} %w_ref), custom_call_target="tpu_custom_call" | custom-call | flops 1048576 | bytes 2097152 | tf_op jit(solution)/shard_map/turn/pallas_call | solution.py:719
  8.2 0.7 pick_y.7
  9.0 2.0 %collective-permute-start.18 = (bf16[272,128]{1,0:T(8,128)(2,1)S(1)}, bf16[272,128]{1,0:T(8,128)(2,1)S(1)}, u32[]{:S(2)}, u32[]{:S(2)}) collective-permute-start(bf16[272,128]{1,0:T(8,128)(2,1)S(1)} %get-tuple-element.162), channel_id=1, source_target_pairs={{0,1},{2,3},{4,5},{6,7},{8,9},{10,11},{12,13},{14,15},{16,17},{18,... | collective-permute-start | bytes 208904 | tf_op jit(solution)/shard_map/ppermute | solution.py:188
  11.0 2.5 %collective-permute-start.19 = (bf16[272,128]{1,0:T(8,128)(2,1)S(1)}, bf16[272,128]{1,0:T(8,128)(2,1)S(1)}, u32[]{:S(2)}, u32[]{:S(2)}) collective-permute-start(bf16[272,128]{1,0:T(8,128)(2,1)S(1)} %get-tuple-element.163), channel_id=1, source_target_pairs={{1,2},{3,4},{5,6},{7,8},{9,10},{11,12},{13,14},{15,16},{17,18},{19... | collective-permute-start | bytes 208904 | tf_op jit(solution)/shard_map/ppermute | solution.py:188
  13.5 3.1 %collective-permute-done.19.yu_ref = bf16[272,128]{1,0:T(8,128)(2,1)S(1)} collective-permute-done((bf16[272,128]{1,0:T(8,128)(2,1)S(1)}, bf16[272,128]{1,0:T(8,128)(2,1)S(1)}, u32[]{:S(2)}, u32[]{:S(2)}) %collective-permute-start.19) | collective-permute-done | bytes 69664 | tf_op jit(solution)/shard_map/ppermute | solution.py:188
  16.6 0.0 copy-start.11
  16.6 0.0 copy-start.13
  16.6 0.0 copy-start.15
  16.6 5.7 %forward_conv.1 = (f32[4,512,128]{2,1,0:T(8,128)S(1)}, bf16[4,640,1152]{2,1,0:T(8,128)(2,1)}, f32[8,128]{1,0:T(8,128)S(1)}) custom-call(s32[3]{0:T(128)S(1)} %pad_add_fusion.place_ref, s32[4,27]{1,0:T(4,128)S(1)} %bitcast.40, s32[4,27]{1,0:T(4,128)S(1)} %bitcast.41, bf16[4,512,128]{2,1,0:T(8,128)(2,1)S(1)} %get-tuple-element.154.own_ref, ...), custom_call_target="tpu_custom_call" | custom-call | flops 6000000000 | bytes 12582912 | tf_op jit(solution)/shard_map/forward_conv/pallas_call | solution.py:322
  22.3 16.4 %all_to_all.57 = f32[16,8,128]{2,1,0:T(8,128)S(1)} all-to-all(f32[16,8,128]{2,1,0:T(8,128)S(1)} %broadcast_in_dim.20), channel_id=1, replica_groups=mesh['xh'=2,'y'=4,'xl'=2,'z'=8,'c'=2] {'z','c'}, dimensions={0} | all-to-all | bytes 131072 | tf_op jit(solution)/shard_map/all_to_all | solution.py:701
  38.7 0.6 broadcast_in_dim.21
  39.4 10.5 %all-to-all-start.11 = ((f32[16,8,128]{2,1,0:T(8,128)}), f32[16,8,128]{2,1,0:T(8,128)S(1)}, u32[]{:S(2)}, u32[]{:S(2)}) async-start(f32[16,8,128]{2,1,0:T(8,128)} %broadcast_in_dim.21), calls=%async_computation.11 | async-start | bytes 131072 | tf_op jit(solution)/shard_map/all_to_all | solution.py:701
  49.9 6.5 %all-to-all-done.11 = f32[16,8,128]{2,1,0:T(8,128)S(1)} async-done(((f32[16,8,128]{2,1,0:T(8,128)}), f32[16,8,128]{2,1,0:T(8,128)S(1)}, u32[]{:S(2)}, u32[]{:S(2)}) %all-to-all-start.11) | async-done | bytes 65568 | tf_op jit(solution)/shard_map/all_to_all | solution.py:701
  56.4 0.6 slice_reduce_fusion
  57.7 85.5 %conditional.1 = (bf16[4,512,128]{2,1,0:T(8,128)(2,1)}, bf16[4,512,128]{2,1,0:T(8,128)(2,1)}, f32[27,128,128]{2,1,0:T(8,128)S(1)}, f32[1,128]{1,0:T(1,128)}, f32[1,128]{1,0:T(1,128)}) conditional(s32[]{:T(128)} %convert_element_type.3, (bf16[1,1,4,512,128]{4,3,2,1,0:T(8,128)(2,1)}, s32[3]{0:T(128)S(1)}, f32[16,8,128]{2,1,0:T(8,128)S(1)}, ...), branch_computations={%region_2.3_spmd, %region_3.5_spmd} | conditional | flops 18012598272 | bytes 130105880 | solution.py:780
  57.8 9.1 %weight_terms.2 = (bf16[4,512,128]{2,1,0:T(8,128)(2,1)}, f32[4,512,128]{2,1,0:T(8,128)S(1)}, f32[8,128]{1,0:T(8,128)S(1)}, f32[3632,128]{1,0:T(8,128)S(1)}, bf16[3632,128]{1,0:T(8,128)(2,1)S(1)}) custom-call(s32[3]{0:T(128)S(1)} %get-tuple-element.48.place_ref, f32[16,8,128]{2,1,0:T(8,128)S(1)} %get-tuple-element.49.stat_ref, ...), custom_call_target="tpu_custom_call" | custom-call | flops 6000000000 | bytes 12582912 | tf_op jit(solution)/shard_map/cond/branch_0_fun/weight_terms/pallas_call | solution.py:532
  66.9 1.7 %collective-permute-start = (bf16[3632,128]{1,0:T(8,128)(2,1)S(1)}, bf16[3632,128]{1,0:T(8,128)(2,1)S(1)}, u32[]{:S(2)}, u32[]{:S(2)}) collective-permute-start(bf16[3632,128]{1,0:T(8,128)(2,1)S(1)} %get-tuple-element.58), channel_id=1, source_target_pairs={{0,1},{1,0},{2,3},{3,2},{4,5},{5,4},{6,7},{7,6},{8,9},{9,8},{10,11... | collective-permute-start | bytes 2789384 | tf_op jit(solution)/shard_map/cond/branch_0_fun/ppermute | solution.py:709
  68.6 2.1 %collective-permute-done.got_ref = bf16[3632,128]{1,0:T(8,128)(2,1)S(1)} collective-permute-done((bf16[3632,128]{1,0:T(8,128)(2,1)S(1)}, bf16[3632,128]{1,0:T(8,128)(2,1)S(1)}, u32[]{:S(2)}, u32[]{:S(2)}) %collective-permute-start) | collective-permute-done | bytes 929824 | tf_op jit(solution)/shard_map/cond/branch_0_fun/ppermute | solution.py:709
  70.7 0.2 join.2
  70.9 0.0 copy-start.6
  70.9 20.2 %all_to_all.50.parts_ref = bf16[16,272,128]{2,1,0:T(8,128)(2,1)S(1)} all-to-all(bf16[16,272,128]{2,1,0:T(8,128)(2,1)S(1)} %join.2), channel_id=1, replica_groups=mesh['xh'=2,'y'=4,'xl'=2,'z'=8,'c'=2] {'xh','y','xl'}, dimensions={0} | all-to-all | bytes 2228224 | tf_op jit(solution)/shard_map/cond/branch_0_fun/all_to_all | solution.py:762
  91.2 0.2 middle.2
  91.4 10.8 %all_to_all.51.parts_ref = f32[8,40,128]{2,1,0:T(8,128)S(1)} all-to-all(f32[8,40,128]{2,1,0:T(8,128)S(1)} %middle.2), channel_id=1, replica_groups=mesh['xh'=2,'y'=4,'xl'=2,'z'=8,'c'=2] {'z'}, dimensions={0} | all-to-all | bytes 327680 | tf_op jit(solution)/shard_map/cond/branch_0_fun/all_to_all | solution.py:763
  102.1 1.1 grad_conv.2
  103.2 0.0 copy-start.9
  103.2 1.3 combine.2
  104.6 3.3 %all-to-all-start.2 = ((bf16[8,16,128]{2,1,0:T(8,128)(2,1)}), bf16[8,16,128]{2,1,0:T(8,128)(2,1)S(1)}, u32[]{:S(2)}, u32[]{:S(2)}) async-start(bf16[8,16,128]{2,1,0:T(8,128)(2,1)} %get-tuple-element.65), calls=%async_computation.2 | async-start | bytes 65536 | tf_op jit(solution)/shard_map/cond/branch_0_fun/all_to_all | solution.py:768
  107.9 0.1 collective-permute-start.1
  108.0 0.7 collective-permute-start.2
  108.7 2.1 %collective-permute-done.1.x1_ref.xl_ref = bf16[2,64,128]{2,1,0:T(8,128)(2,1)S(1)} collective-permute-done((bf16[2,64,128]{2,1,0:T(8,128)(2,1)S(1)}, bf16[2,64,128]{2,1,0:T(8,128)(2,1)S(1)}, u32[]{:S(2)}, u32[]{:S(2)}) %collective-permute-start.1) | collective-permute-done | bytes 32800 | tf_op jit(solution)/shard_map/cond/branch_0_fun/ppermute | solution.py:188
  110.8 0.7 pick_y.4
  111.5 3.2 %all-to-all-done.2 = bf16[8,16,128]{2,1,0:T(8,128)(2,1)S(1)} async-done(((bf16[8,16,128]{2,1,0:T(8,128)(2,1)}), bf16[8,16,128]{2,1,0:T(8,128)(2,1)S(1)}, u32[]{:S(2)}, u32[]{:S(2)}) %all-to-all-start.2) | async-done | bytes 32800 | tf_op jit(solution)/shard_map/cond/branch_0_fun/all_to_all | solution.py:768
  114.7 3.8 %collective-permute-start.3 = (bf16[272,128]{1,0:T(8,128)(2,1)S(1)}, bf16[272,128]{1,0:T(8,128)(2,1)S(1)}, u32[]{:S(2)}, u32[]{:S(2)}) collective-permute-start(bf16[272,128]{1,0:T(8,128)(2,1)S(1)} %get-tuple-element.74), channel_id=1, source_target_pairs={{0,1},{2,3},{4,5},{6,7},{8,9},{10,11},{12,13},{14,15},{16,17},{18,... | collective-permute-start | bytes 208904 | tf_op jit(solution)/shard_map/cond/branch_0_fun/ppermute | solution.py:188
  118.5 2.1 %collective-permute-start.4 = (bf16[272,128]{1,0:T(8,128)(2,1)S(1)}, bf16[272,128]{1,0:T(8,128)(2,1)S(1)}, u32[]{:S(2)}, u32[]{:S(2)}) collective-permute-start(bf16[272,128]{1,0:T(8,128)(2,1)S(1)} %get-tuple-element.75), channel_id=1, source_target_pairs={{1,2},{3,4},{5,6},{7,8},{9,10},{11,12},{13,14},{15,16},{17,18},{19... | collective-permute-start | bytes 208904 | tf_op jit(solution)/shard_map/cond/branch_0_fun/ppermute | solution.py:188
  120.6 0.8 broadcast_in_dim.5
  121.4 6.7 %all-to-all-start.3 = ((bf16[16,112,128]{2,1,0:T(8,128)(2,1)}), bf16[16,112,128]{2,1,0:T(8,128)(2,1)S(1)}, u32[]{:S(2)}, u32[]{:S(2)}) async-start(bf16[16,112,128]{2,1,0:T(8,128)(2,1)} %broadcast_in_dim.5), calls=%async_computation.3 | async-start | bytes 917504 | tf_op jit(solution)/shard_map/cond/branch_0_fun/all_to_all | solution.py:701
  128.2 6.0 %transposed_conv.2 = bf16[4,512,128]{2,1,0:T(8,128)(2,1)} custom-call(s32[3]{0:T(128)S(1)} %get-tuple-element.48.place_ref, s32[4,27]{1,0:T(4,128)S(1)} %get-tuple-element.73.map_ref.rows_ref, s32[4,27]{1,0:T(4,128)S(1)} %get-tuple-element.73.map_ref.rows_ref, bf16[4,512,128]{2,1,0:T(8,128)(2,1)S(1)} %get-tuple-element.67.own_ref, ...), custom_call_target="tpu_custom_call" | custom-call | flops 6000000000 | bytes 12582912 | tf_op jit(solution)/shard_map/cond/branch_0_fun/transposed_conv/pallas_call | solution.py:393
  134.2 2.5 %all-to-all-done.3.mine_ref = bf16[16,112,128]{2,1,0:T(8,128)(2,1)S(1)} async-done(((bf16[16,112,128]{2,1,0:T(8,128)(2,1)}), bf16[16,112,128]{2,1,0:T(8,128)(2,1)S(1)}, u32[]{:S(2)}, u32[]{:S(2)}) %all-to-all-start.3) | async-done | bytes 458784 | tf_op jit(solution)/shard_map/cond/branch_0_fun/all_to_all | solution.py:701
  136.7 3.9 %collective-permute-start.5 = (bf16[16,112,128]{2,1,0:T(8,128)(2,1)S(1)}, bf16[16,112,128]{2,1,0:T(8,128)(2,1)S(1)}, u32[]{:S(2)}, u32[]{:S(2)}) collective-permute-start(bf16[16,112,128]{2,1,0:T(8,128)(2,1)S(1)} %all-to-all-done.3.mine_ref), channel_id=1, source_target_pairs={{0,1},{1,0},{2,3},{3,2},{4,5},{5,4},{6,7},{7,6},{8,9},{9,8},{10,11... | collective-permute-start | bytes 1376264 | tf_op jit(solution)/shard_map/cond/branch_0_fun/ppermute | solution.py:709
  140.6 1.4 collective-permute-done.5.other_ref
  142.1 0.9 finish.2
  143.2 0.0 copy-start.4
  143.2 1.2 copy-done.4
  (29 shorter events, 0.1 us)
Async XLA Ops:
  0.6 15.9 %copy-start.2 = (bf16[27,128,128]{2,1,0:T(8,128)(2,1)S(1)}, bf16[27,128,128]{2,1,0:T(8,128)(2,1)}, u32[]{:S(2)}) copy-start(bf16[27,128,128]{2,1,0:T(8,128)(2,1)} %w_ref) | copy-start | bytes 2654212
  0.6 7.6 %copy-start.12 = (s32[1,1,2,4]{3,2,1,0:T(2,128)S(1)}, s32[1,1,2,4]{3,2,1,0:T(2,128)}, u32[]{:S(2)}) copy-start(s32[1,1,2,4]{3,2,1,0:T(2,128)} %param.17) | copy-start | bytes 100
  0.7 15.9 %copy-start.14 = (s32[1,1,4,27]{3,2,1,0:T(4,128)S(1)}, s32[1,1,4,27]{3,2,1,0:T(4,128)}, u32[]{:S(2)}) copy-start(s32[1,1,4,27]{3,2,1,0:T(4,128)} %param.15) | copy-start | bytes 1300
  2.9 5.3 %collective-permute-start.16 = (bf16[2,64,128]{2,1,0:T(8,128)(2,1)S(1)}, bf16[2,64,128]{2,1,0:T(8,128)(2,1)S(1)}, u32[]{:S(2)}, u32[]{:S(2)}) collective-permute-start(bf16[2,64,128]{2,1,0:T(8,128)(2,1)S(1)} %get-tuple-element.157), channel_id=1, source_target_pairs={{0,32},{64,96},{128,160},{192,224},{32,0},{96,64},{160,128},{224,1... | collective-permute-start | bytes 98312 | tf_op jit(solution)/shard_map/ppermute | solution.py:188
  5.1 3.1 %collective-permute-start.17 = (bf16[2,64,128]{2,1,0:T(8,128)(2,1)S(1)}, bf16[2,64,128]{2,1,0:T(8,128)(2,1)S(1)}, u32[]{:S(2)}, u32[]{:S(2)}) collective-permute-start(bf16[2,64,128]{2,1,0:T(8,128)(2,1)S(1)} %get-tuple-element.158), channel_id=1, source_target_pairs={{32,64},{96,128},{160,192},{64,32},{128,96},{192,160},{33,65},{97,... | collective-permute-start | bytes 98312 | tf_op jit(solution)/shard_map/ppermute | solution.py:188
  9.0 4.5 %collective-permute-start.18 = (bf16[272,128]{1,0:T(8,128)(2,1)S(1)}, bf16[272,128]{1,0:T(8,128)(2,1)S(1)}, u32[]{:S(2)}, u32[]{:S(2)}) collective-permute-start(bf16[272,128]{1,0:T(8,128)(2,1)S(1)} %get-tuple-element.162), channel_id=1, source_target_pairs={{0,1},{2,3},{4,5},{6,7},{8,9},{10,11},{12,13},{14,15},{16,17},{18,... | collective-permute-start | bytes 208904 | tf_op jit(solution)/shard_map/ppermute | solution.py:188
  11.0 5.6 %collective-permute-start.19 = (bf16[272,128]{1,0:T(8,128)(2,1)S(1)}, bf16[272,128]{1,0:T(8,128)(2,1)S(1)}, u32[]{:S(2)}, u32[]{:S(2)}) collective-permute-start(bf16[272,128]{1,0:T(8,128)(2,1)S(1)} %get-tuple-element.163), channel_id=1, source_target_pairs={{1,2},{3,4},{5,6},{7,8},{9,10},{11,12},{13,14},{15,16},{17,18},{19... | collective-permute-start | bytes 208904 | tf_op jit(solution)/shard_map/ppermute | solution.py:188
  16.6 41.1 %copy-start.3 = (bf16[1,1,4,512,128]{4,3,2,1,0:T(8,128)(2,1)S(1)}, bf16[1,1,4,512,128]{4,3,2,1,0:T(8,128)(2,1)}, u32[]{:S(2)}) copy-start(bf16[1,1,4,512,128]{4,3,2,1,0:T(8,128)(2,1)} %param.12) | copy-start | bytes 1572868
  16.6 41.1 %copy-start.10 = (s32[1,1,4,512]{3,2,1,0:T(4,128)S(1)}, s32[1,1,4,512]{3,2,1,0:T(4,128)}, u32[]{:S(2)}) copy-start(s32[1,1,4,512]{3,2,1,0:T(4,128)} %param.13) | copy-start | bytes 24580
  16.6 41.1 %copy-start.11 = (s32[1,1,2,2]{3,2,1,0:T(2,128)S(1)}, s32[1,1,2,2]{3,2,1,0:T(2,128)}, u32[]{:S(2)}) copy-start(s32[1,1,2,2]{3,2,1,0:T(2,128)} %param.16) | copy-start | bytes 52
  16.6 41.1 %copy-start.13 = (f32[128]{0:T(128)S(1)}, f32[128]{0:T(128)}, u32[]{:S(2)}) copy-start(f32[128]{0:T(128)} %param.19) | copy-start | bytes 1540
  16.6 41.1 %copy-start.15 = (f32[128]{0:T(128)S(1)}, f32[128]{0:T(128)}, u32[]{:S(2)}) copy-start(f32[128]{0:T(128)} %param.20) | copy-start | bytes 1540
  39.4 17.0 %all-to-all-start.11 = ((f32[16,8,128]{2,1,0:T(8,128)}), f32[16,8,128]{2,1,0:T(8,128)S(1)}, u32[]{:S(2)}, u32[]{:S(2)}) async-start(f32[16,8,128]{2,1,0:T(8,128)} %broadcast_in_dim.21), calls=%async_computation.11 | async-start | bytes 131072 | tf_op jit(solution)/shard_map/all_to_all | solution.py:701
  57.7 9.2 %copy-start.5 = (f32[4,512,128]{2,1,0:T(8,128)}, f32[4,512,128]{2,1,0:T(8,128)S(1)}, u32[]{:S(2)}) copy-start(f32[4,512,128]{2,1,0:T(8,128)S(1)} %get-tuple-element.50.conv_ref) | copy-start | bytes 3145732 | tf_op jit(solution)/shard_map/cond
  57.8 44.4 %copy-start.8 = (bf16[4,512,128]{2,1,0:T(8,128)(2,1)}, bf16[4,512,128]{2,1,0:T(8,128)(2,1)S(1)}, u32[]{:S(2)}) copy-start(bf16[4,512,128]{2,1,0:T(8,128)(2,1)S(1)} %get-tuple-element.52.mask_ref) | copy-start | bytes 1572868 | tf_op jit(solution)/shard_map/cond
  66.9 3.8 %collective-permute-start = (bf16[3632,128]{1,0:T(8,128)(2,1)S(1)}, bf16[3632,128]{1,0:T(8,128)(2,1)S(1)}, u32[]{:S(2)}, u32[]{:S(2)}) collective-permute-start(bf16[3632,128]{1,0:T(8,128)(2,1)S(1)} %get-tuple-element.58), channel_id=1, source_target_pairs={{0,1},{1,0},{2,3},{3,2},{4,5},{5,4},{6,7},{7,6},{8,9},{9,8},{10,11... | collective-permute-start | bytes 2789384 | tf_op jit(solution)/shard_map/cond/branch_0_fun/ppermute | solution.py:709
  70.9 31.2 %copy-start.6 = (f32[4,512,128]{2,1,0:T(8,128)S(1)}, f32[4,512,128]{2,1,0:T(8,128)}, u32[]{:S(2)}) copy-start(f32[4,512,128]{2,1,0:T(8,128)} %copy-done.5) | copy-start | bytes 3145732 | tf_op jit(solution)/shard_map/cond
  103.2 24.9 %copy-start.7 = (bf16[3,1152,128]{2,1,0:T(8,128)(2,1)S(1)}, bf16[3,1152,128]{2,1,0:T(8,128)(2,1)}, u32[]{:S(2)}) copy-start(bf16[3,1152,128]{2,1,0:T(8,128)(2,1)} %get-tuple-element.76.w_ref) | copy-start | bytes 2654212 | tf_op jit(solution)/shard_map/cond
  103.2 24.9 %copy-start.9 = (bf16[4,512,128]{2,1,0:T(8,128)(2,1)S(1)}, bf16[4,512,128]{2,1,0:T(8,128)(2,1)}, u32[]{:S(2)}) copy-start(bf16[4,512,128]{2,1,0:T(8,128)(2,1)} %copy-done.8) | copy-start | bytes 1572868 | tf_op jit(solution)/shard_map/cond
  104.6 10.1 %all-to-all-start.2 = ((bf16[8,16,128]{2,1,0:T(8,128)(2,1)}), bf16[8,16,128]{2,1,0:T(8,128)(2,1)S(1)}, u32[]{:S(2)}, u32[]{:S(2)}) async-start(bf16[8,16,128]{2,1,0:T(8,128)(2,1)} %get-tuple-element.65), calls=%async_computation.2 | async-start | bytes 65536 | tf_op jit(solution)/shard_map/cond/branch_0_fun/all_to_all | solution.py:768
  107.9 2.9 %collective-permute-start.1 = (bf16[2,64,128]{2,1,0:T(8,128)(2,1)S(1)}, bf16[2,64,128]{2,1,0:T(8,128)(2,1)S(1)}, u32[]{:S(2)}, u32[]{:S(2)}) collective-permute-start(bf16[2,64,128]{2,1,0:T(8,128)(2,1)S(1)} %get-tuple-element.68), channel_id=1, source_target_pairs={{0,32},{64,96},{128,160},{192,224},{32,0},{96,64},{160,128},{224,1... | collective-permute-start | bytes 98312 | tf_op jit(solution)/shard_map/cond/branch_0_fun/ppermute | solution.py:188
  108.0 2.8 %collective-permute-start.2 = (bf16[2,64,128]{2,1,0:T(8,128)(2,1)S(1)}, bf16[2,64,128]{2,1,0:T(8,128)(2,1)S(1)}, u32[]{:S(2)}, u32[]{:S(2)}) collective-permute-start(bf16[2,64,128]{2,1,0:T(8,128)(2,1)S(1)} %get-tuple-element.69), channel_id=1, source_target_pairs={{32,64},{96,128},{160,192},{64,32},{128,96},{192,160},{33,65},{97,... | collective-permute-start | bytes 98312 | tf_op jit(solution)/shard_map/cond/branch_0_fun/ppermute | solution.py:188
  114.7 13.4 %collective-permute-start.3 = (bf16[272,128]{1,0:T(8,128)(2,1)S(1)}, bf16[272,128]{1,0:T(8,128)(2,1)S(1)}, u32[]{:S(2)}, u32[]{:S(2)}) collective-permute-start(bf16[272,128]{1,0:T(8,128)(2,1)S(1)} %get-tuple-element.74), channel_id=1, source_target_pairs={{0,1},{2,3},{4,5},{6,7},{8,9},{10,11},{12,13},{14,15},{16,17},{18,... | collective-permute-start | bytes 208904 | tf_op jit(solution)/shard_map/cond/branch_0_fun/ppermute | solution.py:188
  118.5 9.6 %collective-permute-start.4 = (bf16[272,128]{1,0:T(8,128)(2,1)S(1)}, bf16[272,128]{1,0:T(8,128)(2,1)S(1)}, u32[]{:S(2)}, u32[]{:S(2)}) collective-permute-start(bf16[272,128]{1,0:T(8,128)(2,1)S(1)} %get-tuple-element.75), channel_id=1, source_target_pairs={{1,2},{3,4},{5,6},{7,8},{9,10},{11,12},{13,14},{15,16},{17,18},{19... | collective-permute-start | bytes 208904 | tf_op jit(solution)/shard_map/cond/branch_0_fun/ppermute | solution.py:188
  121.4 15.3 %all-to-all-start.3 = ((bf16[16,112,128]{2,1,0:T(8,128)(2,1)}), bf16[16,112,128]{2,1,0:T(8,128)(2,1)S(1)}, u32[]{:S(2)}, u32[]{:S(2)}) async-start(bf16[16,112,128]{2,1,0:T(8,128)(2,1)} %broadcast_in_dim.5), calls=%async_computation.3 | async-start | bytes 917504 | tf_op jit(solution)/shard_map/cond/branch_0_fun/all_to_all | solution.py:701
  136.7 5.4 %collective-permute-start.5 = (bf16[16,112,128]{2,1,0:T(8,128)(2,1)S(1)}, bf16[16,112,128]{2,1,0:T(8,128)(2,1)S(1)}, u32[]{:S(2)}, u32[]{:S(2)}) collective-permute-start(bf16[16,112,128]{2,1,0:T(8,128)(2,1)S(1)} %all-to-all-done.3.mine_ref), channel_id=1, source_target_pairs={{0,1},{1,0},{2,3},{3,2},{4,5},{5,4},{6,7},{7,6},{8,9},{9,8},{10,11... | collective-permute-start | bytes 1376264 | tf_op jit(solution)/shard_map/cond/branch_0_fun/ppermute | solution.py:709
  143.2 1.2 copy-start.4

commit v2 on v1

--- a/solution.py
+++ b/solution.py
@@ -40,12 +40,12 @@
 
 
 def side_of(turn, odd):
-    return odd if turn else 1 - odd
+    return 1 - odd if turn else odd
 
 
 def lower_upper(odd, first, second):
     even = odd == 0
-    return jnp.where(even, second, first), jnp.where(even, first, second)
+    return jnp.where(even, first, second), jnp.where(even, second, first)
 
 
 def pick_x(place_ref, sends_ref, own_ref, first_ref, second_ref, faces):
@@ -183,7 +183,7 @@
 def neighbours(first, second, axes, faces):
     size = axis_size(axes)
     if faces:
-        pairs = [[(i, i + 1) for i in range(turn, size - 1, 2)] for turn in (0, 1)]
+        pairs = [[(i, i + 1) for i in range(1 - turn, size - 1, 2)] for turn in (0, 1)]
         one, two = [pair + [(j, i) for i, j in pair] for pair in pairs]
         return lax.ppermute(first, axes, one), lax.ppermute(second, axes, two)
     up = [(i, i + 1) for i in range(size - 1)]

time: 145 us -> 143 us (0.986)
  waiting for transfers between devices: 21 us -> 19.1 us
    ppermute x8, starting transfers between devices: 14 us -> 18.8 us  [neighbours(): return (lax.ppermute(first, axes, one), lax.ppermute(second, axes, two))]
    all_to_all x2, starting transfers between devices: 17.2 us -> 13 us  [spread(): lax.all_to_all(jnp.broadcast_to(value[None], (size,) + value.shape), axes...]
    ppermute x8, waiting for transfers between devices: 5.19 us -> 3.2 us  [neighbours(): return (lax.ppermute(first, axes, one), lax.ppermute(second, axes, two))]
    ppermute x2, starting transfers between devices: 5.62 us -> 3.64 us  [swap(): return lax.ppermute(value, 'c', [(0, 1), (1, 0)])]
where the time goes in v2:
time: 143 us; the launch traced here: 142 us
  blocking collectives  48.5 us (34%)
  starting transfers between devices  38.8 us (27%)
  Pallas kernels  29.9 us (21%)
  waiting for transfers between devices  19.1 us (13%)
  local copies, waits for them, and re-layouts  2.75 us (2%)
  between operations  2.22 us (2%)
    all_to_all x1, blocking collectives, second(): parts = lax.all_to_all(join(keep, swap(send)), CROSS, 0, 0)  20.2 us
    ppermute x8, starting transfers between devices, neighbours(): return (lax.ppermute(first, axes, one), lax.ppermute(second, axes, two))  18.8 us
    all_to_all x1, blocking collectives, spread(): lax.all_to_all(jnp.broadcast_to(value[None], (size,) + value.shape), axes...  17.5 us
    all_to_all x2, starting transfers between devices, spread(): lax.all_to_all(jnp.broadcast_to(value[None], (size,) + value.shape), axes...  13 us
    all_to_all x1, blocking collectives, second(): parts = lax.all_to_all(middle(parts), 'z', 0, 0)  10.8 us
    all_to_all x2, waiting for transfers between devices, spread(): lax.all_to_all(jnp.broadcast_to(value[None], (size,) + value.shape), axes...  10.2 us
    pallas_call x1, Pallas kernels, wgrad(): pl.pallas_call(functools.partial(wgrad_kernel, unroll=unroll), out_shape=...  9.14 us
    pallas_call x1, Pallas kernels, conv_steps(): pl.pallas_call(functools.partial(step_kernel, forward=forward, faces=face...  6.01 us
  transfers between devices with their start and end apart: 13, of which 7 were waited for; matrix products, arithmetic and copies ran while one was open for 1% of the time, Pallas kernels for 6%

profile of v2, /device:TPU:1, one launch (start us, length us, event | category | flops | bytes accessed | tf_op | source)
XLA Modules:
  0.0 142.3 jit_solution(3918846458543509004)
XLA Ops:
  0.6 0.0 copy-start.2
  1.4 0.1 pad_add_fusion.place_ref
  1.5 1.4 prepare.3
  2.9 0.7 collective-permute-start.16
  3.6 4.8 %collective-permute-start.17 = (bf16[2,64,128]{2,1,0:T(8,128)(2,1)S(1)}, bf16[2,64,128]{2,1,0:T(8,128)(2,1)S(1)}, u32[]{:S(2)}, u32[]{:S(2)}) collective-permute-start(bf16[2,64,128]{2,1,0:T(8,128)(2,1)S(1)} %get-tuple-element.158), channel_id=1, source_target_pairs={{0,32},{64,96},{128,160},{192,224},{32,0},{96,64},{160,128},{224,1... | collective-permute-start | bytes 98312 | tf_op jit(solution)/shard_map/ppermute | solution.py:188
  8.3 2.5 %turn.3 = bf16[3,1152,128]{2,1,0:T(8,128)(2,1)} custom-call(bf16[27,128,128]{2,1,0:T(8,128)(2,1)} %w_ref), custom_call_target="tpu_custom_call" | custom-call | flops 1048576 | bytes 2097152 | tf_op jit(solution)/shard_map/turn/pallas_call | solution.py:719
  10.8 0.8 pick_y.7
  11.5 4.7 %collective-permute-start.18 = (bf16[272,128]{1,0:T(8,128)(2,1)S(1)}, bf16[272,128]{1,0:T(8,128)(2,1)S(1)}, u32[]{:S(2)}, u32[]{:S(2)}) collective-permute-start(bf16[272,128]{1,0:T(8,128)(2,1)S(1)} %get-tuple-element.162), channel_id=1, source_target_pairs={{1,2},{3,4},{5,6},{7,8},{9,10},{11,12},{13,14},{15,16},{17,18},{19... | collective-permute-start | bytes 208904 | tf_op jit(solution)/shard_map/ppermute | solution.py:188
  16.2 0.1 collective-permute-start.19
  16.3 1.9 %collective-permute-done.18.yl_ref = bf16[272,128]{1,0:T(8,128)(2,1)S(1)} collective-permute-done((bf16[272,128]{1,0:T(8,128)(2,1)S(1)}, bf16[272,128]{1,0:T(8,128)(2,1)S(1)}, u32[]{:S(2)}, u32[]{:S(2)}) %collective-permute-start.18) | collective-permute-done | bytes 69664 | tf_op jit(solution)/shard_map/ppermute | solution.py:188
  18.2 0.0 copy-start.10
  18.3 0.0 copy-start.11
  18.3 5.7 %forward_conv.1 = (f32[4,512,128]{2,1,0:T(8,128)S(1)}, bf16[4,640,1152]{2,1,0:T(8,128)(2,1)}, f32[8,128]{1,0:T(8,128)S(1)}) custom-call(s32[3]{0:T(128)S(1)} %pad_add_fusion.place_ref, s32[4,27]{1,0:T(4,128)S(1)} %bitcast.40, s32[4,27]{1,0:T(4,128)S(1)} %bitcast.41, bf16[4,512,128]{2,1,0:T(8,128)(2,1)S(1)} %get-tuple-element.154.own_ref, ...), custom_call_target="tpu_custom_call" | custom-call | flops 6000000000 | bytes 12582912 | tf_op jit(solution)/shard_map/forward_conv/pallas_call | solution.py:322
  24.0 17.5 %all_to_all.57 = f32[16,8,128]{2,1,0:T(8,128)S(1)} all-to-all(f32[16,8,128]{2,1,0:T(8,128)S(1)} %broadcast_in_dim.20), channel_id=1, replica_groups=mesh['xh'=2,'y'=4,'xl'=2,'z'=8,'c'=2] {'z','c'}, dimensions={0} | all-to-all | bytes 131072 | tf_op jit(solution)/shard_map/all_to_all | solution.py:701
  41.5 0.6 broadcast_in_dim.21
  42.1 6.8 %all-to-all-start.11 = ((f32[16,8,128]{2,1,0:T(8,128)}), f32[16,8,128]{2,1,0:T(8,128)S(1)}, u32[]{:S(2)}, u32[]{:S(2)}) async-start(f32[16,8,128]{2,1,0:T(8,128)} %broadcast_in_dim.21), calls=%async_computation.11 | async-start | bytes 131072 | tf_op jit(solution)/shard_map/all_to_all | solution.py:701
  49.0 6.5 %all-to-all-done.11 = f32[16,8,128]{2,1,0:T(8,128)S(1)} async-done(((f32[16,8,128]{2,1,0:T(8,128)}), f32[16,8,128]{2,1,0:T(8,128)S(1)}, u32[]{:S(2)}, u32[]{:S(2)}) %all-to-all-start.11) | async-done | bytes 65568 | tf_op jit(solution)/shard_map/all_to_all | solution.py:701
  55.5 0.6 slice_reduce_fusion
  56.8 84.2 %conditional.1 = (bf16[4,512,128]{2,1,0:T(8,128)(2,1)}, bf16[4,512,128]{2,1,0:T(8,128)(2,1)}, f32[27,128,128]{2,1,0:T(8,128)S(1)}, f32[1,128]{1,0:T(1,128)}, f32[1,128]{1,0:T(1,128)}) conditional(s32[]{:T(128)} %convert_element_type.3, (bf16[1,1,4,512,128]{4,3,2,1,0:T(8,128)(2,1)}, s32[3]{0:T(128)S(1)}, f32[16,8,128]{2,1,0:T(8,128)S(1)}, ...), branch_computations={%region_2.3_spmd, %region_3.5_spmd} | conditional | flops 18012598272 | bytes 130105880 | solution.py:780
  56.8 0.0 copy-start.5
  56.8 0.0 copy-start.8
  56.8 9.1 %weight_terms.2 = (bf16[4,512,128]{2,1,0:T(8,128)(2,1)}, f32[4,512,128]{2,1,0:T(8,128)S(1)}, f32[8,128]{1,0:T(8,128)S(1)}, f32[3632,128]{1,0:T(8,128)S(1)}, bf16[3632,128]{1,0:T(8,128)(2,1)S(1)}) custom-call(s32[3]{0:T(128)S(1)} %get-tuple-element.48.place_ref, f32[16,8,128]{2,1,0:T(8,128)S(1)} %get-tuple-element.49.stat_ref, ...), custom_call_target="tpu_custom_call" | custom-call | flops 6000000000 | bytes 12582912 | tf_op jit(solution)/shard_map/cond/branch_0_fun/weight_terms/pallas_call | solution.py:532
  66.0 1.7 %collective-permute-start = (bf16[3632,128]{1,0:T(8,128)(2,1)S(1)}, bf16[3632,128]{1,0:T(8,128)(2,1)S(1)}, u32[]{:S(2)}, u32[]{:S(2)}) collective-permute-start(bf16[3632,128]{1,0:T(8,128)(2,1)S(1)} %get-tuple-element.58), channel_id=1, source_target_pairs={{0,1},{1,0},{2,3},{3,2},{4,5},{5,4},{6,7},{7,6},{8,9},{9,8},{10,11... | collective-permute-start | bytes 2789384 | tf_op jit(solution)/shard_map/cond/branch_0_fun/ppermute | solution.py:709
  67.7 2.1 %collective-permute-done.got_ref = bf16[3632,128]{1,0:T(8,128)(2,1)S(1)} collective-permute-done((bf16[3632,128]{1,0:T(8,128)(2,1)S(1)}, bf16[3632,128]{1,0:T(8,128)(2,1)S(1)}, u32[]{:S(2)}, u32[]{:S(2)}) %collective-permute-start) | collective-permute-done | bytes 929824 | tf_op jit(solution)/shard_map/cond/branch_0_fun/ppermute | solution.py:709
  69.8 0.2 join.2
  70.0 0.0 copy-start.6
  70.0 20.2 %all_to_all.50.parts_ref = bf16[16,272,128]{2,1,0:T(8,128)(2,1)S(1)} all-to-all(bf16[16,272,128]{2,1,0:T(8,128)(2,1)S(1)} %join.2), channel_id=1, replica_groups=mesh['xh'=2,'y'=4,'xl'=2,'z'=8,'c'=2] {'xh','y','xl'}, dimensions={0} | all-to-all | bytes 2228224 | tf_op jit(solution)/shard_map/cond/branch_0_fun/all_to_all | solution.py:762
  90.2 0.2 middle.2
  90.4 10.8 %all_to_all.51.parts_ref = f32[8,40,128]{2,1,0:T(8,128)S(1)} all-to-all(f32[8,40,128]{2,1,0:T(8,128)S(1)} %middle.2), channel_id=1, replica_groups=mesh['xh'=2,'y'=4,'xl'=2,'z'=8,'c'=2] {'z'}, dimensions={0} | all-to-all | bytes 327680 | tf_op jit(solution)/shard_map/cond/branch_0_fun/all_to_all | solution.py:763
  101.2 1.1 grad_conv.2
  102.3 1.3 combine.2
  103.6 3.3 %all-to-all-start.2 = ((bf16[8,16,128]{2,1,0:T(8,128)(2,1)}), bf16[8,16,128]{2,1,0:T(8,128)(2,1)S(1)}, u32[]{:S(2)}, u32[]{:S(2)}) async-start(bf16[8,16,128]{2,1,0:T(8,128)(2,1)} %get-tuple-element.65), calls=%async_computation.2 | async-start | bytes 65536 | tf_op jit(solution)/shard_map/cond/branch_0_fun/all_to_all | solution.py:768
  107.0 0.7 collective-permute-start.1
  107.6 2.0 %collective-permute-start.2 = (bf16[2,64,128]{2,1,0:T(8,128)(2,1)S(1)}, bf16[2,64,128]{2,1,0:T(8,128)(2,1)S(1)}, u32[]{:S(2)}, u32[]{:S(2)}) collective-permute-start(bf16[2,64,128]{2,1,0:T(8,128)(2,1)S(1)} %get-tuple-element.69), channel_id=1, source_target_pairs={{0,32},{64,96},{128,160},{192,224},{32,0},{96,64},{160,128},{224,1... | collective-permute-start | bytes 98312 | tf_op jit(solution)/shard_map/cond/branch_0_fun/ppermute | solution.py:188
  109.6 1.3 collective-permute-done.2.x2_ref.xu_ref
  110.9 0.8 pick_y.4
  111.7 2.1 %all-to-all-done.2 = bf16[8,16,128]{2,1,0:T(8,128)(2,1)S(1)} async-done(((bf16[8,16,128]{2,1,0:T(8,128)(2,1)}), bf16[8,16,128]{2,1,0:T(8,128)(2,1)S(1)}, u32[]{:S(2)}, u32[]{:S(2)}) %all-to-all-start.2) | async-done | bytes 32800 | tf_op jit(solution)/shard_map/cond/branch_0_fun/all_to_all | solution.py:768
  113.8 5.9 %collective-permute-start.3 = (bf16[272,128]{1,0:T(8,128)(2,1)S(1)}, bf16[272,128]{1,0:T(8,128)(2,1)S(1)}, u32[]{:S(2)}, u32[]{:S(2)}) collective-permute-start(bf16[272,128]{1,0:T(8,128)(2,1)S(1)} %get-tuple-element.74), channel_id=1, source_target_pairs={{1,2},{3,4},{5,6},{7,8},{9,10},{11,12},{13,14},{15,16},{17,18},{19... | collective-permute-start | bytes 208904 | tf_op jit(solution)/shard_map/cond/branch_0_fun/ppermute | solution.py:188
  119.7 0.1 collective-permute-start.4
  119.8 0.8 broadcast_in_dim.5
  120.6 6.1 %all-to-all-start.3 = ((bf16[16,112,128]{2,1,0:T(8,128)(2,1)}), bf16[16,112,128]{2,1,0:T(8,128)(2,1)S(1)}, u32[]{:S(2)}, u32[]{:S(2)}) async-start(bf16[16,112,128]{2,1,0:T(8,128)(2,1)} %broadcast_in_dim.5), calls=%async_computation.3 | async-start | bytes 917504 | tf_op jit(solution)/shard_map/cond/branch_0_fun/all_to_all | solution.py:701
  126.8 6.0 %transposed_conv.2 = bf16[4,512,128]{2,1,0:T(8,128)(2,1)} custom-call(s32[3]{0:T(128)S(1)} %get-tuple-element.48.place_ref, s32[4,27]{1,0:T(4,128)S(1)} %get-tuple-element.73.map_ref.rows_ref, s32[4,27]{1,0:T(4,128)S(1)} %get-tuple-element.73.map_ref.rows_ref, bf16[4,512,128]{2,1,0:T(8,128)(2,1)S(1)} %get-tuple-element.67.own_ref, ...), custom_call_target="tpu_custom_call" | custom-call | flops 6000000000 | bytes 12582912 | tf_op jit(solution)/shard_map/cond/branch_0_fun/transposed_conv/pallas_call | solution.py:393
  132.8 3.7 %all-to-all-done.3.mine_ref = bf16[16,112,128]{2,1,0:T(8,128)(2,1)S(1)} async-done(((bf16[16,112,128]{2,1,0:T(8,128)(2,1)}), bf16[16,112,128]{2,1,0:T(8,128)(2,1)S(1)}, u32[]{:S(2)}, u32[]{:S(2)}) %all-to-all-start.3) | async-done | bytes 458784 | tf_op jit(solution)/shard_map/cond/branch_0_fun/all_to_all | solution.py:701
  136.5 2.0 %collective-permute-start.5 = (bf16[16,112,128]{2,1,0:T(8,128)(2,1)S(1)}, bf16[16,112,128]{2,1,0:T(8,128)(2,1)S(1)}, u32[]{:S(2)}, u32[]{:S(2)}) collective-permute-start(bf16[16,112,128]{2,1,0:T(8,128)(2,1)S(1)} %all-to-all-done.3.mine_ref), channel_id=1, source_target_pairs={{0,1},{1,0},{2,3},{3,2},{4,5},{5,4},{6,7},{7,6},{8,9},{9,8},{10,11... | collective-permute-start | bytes 1376264 | tf_op jit(solution)/shard_map/cond/branch_0_fun/ppermute | solution.py:709
  138.5 1.4 %collective-permute-done.5.other_ref = bf16[16,112,128]{2,1,0:T(8,128)(2,1)S(1)} collective-permute-done((bf16[16,112,128]{2,1,0:T(8,128)(2,1)S(1)}, bf16[16,112,128]{2,1,0:T(8,128)(2,1)S(1)}, u32[]{:S(2)}, u32[]{:S(2)}) %collective-permute-start.5) | collective-permute-done | bytes 458784 | tf_op jit(solution)/shard_map/cond/branch_0_fun/ppermute | solution.py:709
  139.9 0.9 finish.2
  141.0 0.0 copy-start.4
  141.1 1.2 copy-done.4
  (29 shorter events, 0.1 us)
Async XLA Ops:
  0.6 17.6 %copy-start.2 = (bf16[27,128,128]{2,1,0:T(8,128)(2,1)S(1)}, bf16[27,128,128]{2,1,0:T(8,128)(2,1)}, u32[]{:S(2)}) copy-start(bf16[27,128,128]{2,1,0:T(8,128)(2,1)} %w_ref) | copy-start | bytes 2654212
  0.6 10.1 %copy-start.12 = (s32[1,1,2,4]{3,2,1,0:T(2,128)S(1)}, s32[1,1,2,4]{3,2,1,0:T(2,128)}, u32[]{:S(2)}) copy-start(s32[1,1,2,4]{3,2,1,0:T(2,128)} %param.17) | copy-start | bytes 100
  0.7 17.6 %copy-start.14 = (s32[1,1,4,27]{3,2,1,0:T(4,128)S(1)}, s32[1,1,4,27]{3,2,1,0:T(4,128)}, u32[]{:S(2)}) copy-start(s32[1,1,4,27]{3,2,1,0:T(4,128)} %param.15) | copy-start | bytes 1300
  2.9 7.9 %collective-permute-start.16 = (bf16[2,64,128]{2,1,0:T(8,128)(2,1)S(1)}, bf16[2,64,128]{2,1,0:T(8,128)(2,1)S(1)}, u32[]{:S(2)}, u32[]{:S(2)}) collective-permute-start(bf16[2,64,128]{2,1,0:T(8,128)(2,1)S(1)} %get-tuple-element.157), channel_id=1, source_target_pairs={{32,64},{96,128},{160,192},{64,32},{128,96},{192,160},{33,65},{97,... | collective-permute-start | bytes 98312 | tf_op jit(solution)/shard_map/ppermute | solution.py:188
  3.6 7.2 %collective-permute-start.17 = (bf16[2,64,128]{2,1,0:T(8,128)(2,1)S(1)}, bf16[2,64,128]{2,1,0:T(8,128)(2,1)S(1)}, u32[]{:S(2)}, u32[]{:S(2)}) collective-permute-start(bf16[2,64,128]{2,1,0:T(8,128)(2,1)S(1)} %get-tuple-element.158), channel_id=1, source_target_pairs={{0,32},{64,96},{128,160},{192,224},{32,0},{96,64},{160,128},{224,1... | collective-permute-start | bytes 98312 | tf_op jit(solution)/shard_map/ppermute | solution.py:188
  11.5 6.7 %collective-permute-start.18 = (bf16[272,128]{1,0:T(8,128)(2,1)S(1)}, bf16[272,128]{1,0:T(8,128)(2,1)S(1)}, u32[]{:S(2)}, u32[]{:S(2)}) collective-permute-start(bf16[272,128]{1,0:T(8,128)(2,1)S(1)} %get-tuple-element.162), channel_id=1, source_target_pairs={{1,2},{3,4},{5,6},{7,8},{9,10},{11,12},{13,14},{15,16},{17,18},{19... | collective-permute-start | bytes 208904 | tf_op jit(solution)/shard_map/ppermute | solution.py:188
  16.2 2.0 %collective-permute-start.19 = (bf16[272,128]{1,0:T(8,128)(2,1)S(1)}, bf16[272,128]{1,0:T(8,128)(2,1)S(1)}, u32[]{:S(2)}, u32[]{:S(2)}) collective-permute-start(bf16[272,128]{1,0:T(8,128)(2,1)S(1)} %get-tuple-element.163), channel_id=1, source_target_pairs={{0,1},{2,3},{4,5},{6,7},{8,9},{10,11},{12,13},{14,15},{16,17},{18,... | collective-permute-start | bytes 208904 | tf_op jit(solution)/shard_map/ppermute | solution.py:188
  18.2 38.5 %copy-start.3 = (bf16[1,1,4,512,128]{4,3,2,1,0:T(8,128)(2,1)S(1)}, bf16[1,1,4,512,128]{4,3,2,1,0:T(8,128)(2,1)}, u32[]{:S(2)}) copy-start(bf16[1,1,4,512,128]{4,3,2,1,0:T(8,128)(2,1)} %param.12) | copy-start | bytes 1572868
  18.2 38.5 %copy-start.10 = (s32[1,1,4,512]{3,2,1,0:T(4,128)S(1)}, s32[1,1,4,512]{3,2,1,0:T(4,128)}, u32[]{:S(2)}) copy-start(s32[1,1,4,512]{3,2,1,0:T(4,128)} %param.13) | copy-start | bytes 24580
  18.3 38.5 %copy-start.11 = (s32[1,1,2,2]{3,2,1,0:T(2,128)S(1)}, s32[1,1,2,2]{3,2,1,0:T(2,128)}, u32[]{:S(2)}) copy-start(s32[1,1,2,2]{3,2,1,0:T(2,128)} %param.16) | copy-start | bytes 52
  18.3 38.5 %copy-start.13 = (f32[128]{0:T(128)S(1)}, f32[128]{0:T(128)}, u32[]{:S(2)}) copy-start(f32[128]{0:T(128)} %param.19) | copy-start | bytes 1540
  18.3 38.5 %copy-start.15 = (f32[128]{0:T(128)S(1)}, f32[128]{0:T(128)}, u32[]{:S(2)}) copy-start(f32[128]{0:T(128)} %param.20) | copy-start | bytes 1540
  42.1 13.4 %all-to-all-start.11 = ((f32[16,8,128]{2,1,0:T(8,128)}), f32[16,8,128]{2,1,0:T(8,128)S(1)}, u32[]{:S(2)}, u32[]{:S(2)}) async-start(f32[16,8,128]{2,1,0:T(8,128)} %broadcast_in_dim.21), calls=%async_computation.11 | async-start | bytes 131072 | tf_op jit(solution)/shard_map/all_to_all | solution.py:701
  56.8 9.2 %copy-start.5 = (f32[4,512,128]{2,1,0:T(8,128)}, f32[4,512,128]{2,1,0:T(8,128)S(1)}, u32[]{:S(2)}) copy-start(f32[4,512,128]{2,1,0:T(8,128)S(1)} %get-tuple-element.50.conv_ref) | copy-start | bytes 3145732 | tf_op jit(solution)/shard_map/cond
  56.8 44.4 %copy-start.8 = (bf16[4,512,128]{2,1,0:T(8,128)(2,1)}, bf16[4,512,128]{2,1,0:T(8,128)(2,1)S(1)}, u32[]{:S(2)}) copy-start(bf16[4,512,128]{2,1,0:T(8,128)(2,1)S(1)} %get-tuple-element.52.mask_ref) | copy-start | bytes 1572868 | tf_op jit(solution)/shard_map/cond
  66.0 3.8 %collective-permute-start = (bf16[3632,128]{1,0:T(8,128)(2,1)S(1)}, bf16[3632,128]{1,0:T(8,128)(2,1)S(1)}, u32[]{:S(2)}, u32[]{:S(2)}) collective-permute-start(bf16[3632,128]{1,0:T(8,128)(2,1)S(1)} %get-tuple-element.58), channel_id=1, source_target_pairs={{0,1},{1,0},{2,3},{3,2},{4,5},{5,4},{6,7},{7,6},{8,9},{9,8},{10,11... | collective-permute-start | bytes 2789384 | tf_op jit(solution)/shard_map/cond/branch_0_fun/ppermute | solution.py:709
  70.0 31.2 %copy-start.6 = (f32[4,512,128]{2,1,0:T(8,128)S(1)}, f32[4,512,128]{2,1,0:T(8,128)}, u32[]{:S(2)}) copy-start(f32[4,512,128]{2,1,0:T(8,128)} %copy-done.5) | copy-start | bytes 3145732 | tf_op jit(solution)/shard_map/cond
  102.3 24.5 %copy-start.7 = (bf16[3,1152,128]{2,1,0:T(8,128)(2,1)S(1)}, bf16[3,1152,128]{2,1,0:T(8,128)(2,1)}, u32[]{:S(2)}) copy-start(bf16[3,1152,128]{2,1,0:T(8,128)(2,1)} %get-tuple-element.76.w_ref) | copy-start | bytes 2654212 | tf_op jit(solution)/shard_map/cond
  102.3 24.5 %copy-start.9 = (bf16[4,512,128]{2,1,0:T(8,128)(2,1)S(1)}, bf16[4,512,128]{2,1,0:T(8,128)(2,1)}, u32[]{:S(2)}) copy-start(bf16[4,512,128]{2,1,0:T(8,128)(2,1)} %copy-done.8) | copy-start | bytes 1572868 | tf_op jit(solution)/shard_map/cond
  103.6 10.1 %all-to-all-start.2 = ((bf16[8,16,128]{2,1,0:T(8,128)(2,1)}), bf16[8,16,128]{2,1,0:T(8,128)(2,1)S(1)}, u32[]{:S(2)}, u32[]{:S(2)}) async-start(bf16[8,16,128]{2,1,0:T(8,128)(2,1)} %get-tuple-element.65), calls=%async_computation.2 | async-start | bytes 65536 | tf_op jit(solution)/shard_map/cond/branch_0_fun/all_to_all | solution.py:768
  107.0 2.7 %collective-permute-start.1 = (bf16[2,64,128]{2,1,0:T(8,128)(2,1)S(1)}, bf16[2,64,128]{2,1,0:T(8,128)(2,1)S(1)}, u32[]{:S(2)}, u32[]{:S(2)}) collective-permute-start(bf16[2,64,128]{2,1,0:T(8,128)(2,1)S(1)} %get-tuple-element.68), channel_id=1, source_target_pairs={{32,64},{96,128},{160,192},{64,32},{128,96},{192,160},{33,65},{97,... | collective-permute-start | bytes 98312 | tf_op jit(solution)/shard_map/cond/branch_0_fun/ppermute | solution.py:188
  107.6 3.3 %collective-permute-start.2 = (bf16[2,64,128]{2,1,0:T(8,128)(2,1)S(1)}, bf16[2,64,128]{2,1,0:T(8,128)(2,1)S(1)}, u32[]{:S(2)}, u32[]{:S(2)}) collective-permute-start(bf16[2,64,128]{2,1,0:T(8,128)(2,1)S(1)} %get-tuple-element.69), channel_id=1, source_target_pairs={{0,32},{64,96},{128,160},{192,224},{32,0},{96,64},{160,128},{224,1... | collective-permute-start | bytes 98312 | tf_op jit(solution)/shard_map/cond/branch_0_fun/ppermute | solution.py:188
  113.8 13.0 %collective-permute-start.3 = (bf16[272,128]{1,0:T(8,128)(2,1)S(1)}, bf16[272,128]{1,0:T(8,128)(2,1)S(1)}, u32[]{:S(2)}, u32[]{:S(2)}) collective-permute-start(bf16[272,128]{1,0:T(8,128)(2,1)S(1)} %get-tuple-element.74), channel_id=1, source_target_pairs={{1,2},{3,4},{5,6},{7,8},{9,10},{11,12},{13,14},{15,16},{17,18},{19... | collective-permute-start | bytes 208904 | tf_op jit(solution)/shard_map/cond/branch_0_fun/ppermute | solution.py:188
  119.7 7.1 %collective-permute-start.4 = (bf16[272,128]{1,0:T(8,128)(2,1)S(1)}, bf16[272,128]{1,0:T(8,128)(2,1)S(1)}, u32[]{:S(2)}, u32[]{:S(2)}) collective-permute-start(bf16[272,128]{1,0:T(8,128)(2,1)S(1)} %get-tuple-element.75), channel_id=1, source_target_pairs={{0,1},{2,3},{4,5},{6,7},{8,9},{10,11},{12,13},{14,15},{16,17},{18,... | collective-permute-start | bytes 208904 | tf_op jit(solution)/shard_map/cond/branch_0_fun/ppermute | solution.py:188
  120.6 15.9 %all-to-all-start.3 = ((bf16[16,112,128]{2,1,0:T(8,128)(2,1)}), bf16[16,112,128]{2,1,0:T(8,128)(2,1)S(1)}, u32[]{:S(2)}, u32[]{:S(2)}) async-start(bf16[16,112,128]{2,1,0:T(8,128)(2,1)} %broadcast_in_dim.5), calls=%async_computation.3 | async-start | bytes 917504 | tf_op jit(solution)/shard_map/cond/branch_0_fun/all_to_all | solution.py:701
  136.5 3.4 %collective-permute-start.5 = (bf16[16,112,128]{2,1,0:T(8,128)(2,1)S(1)}, bf16[16,112,128]{2,1,0:T(8,128)(2,1)S(1)}, u32[]{:S(2)}, u32[]{:S(2)}) collective-permute-start(bf16[16,112,128]{2,1,0:T(8,128)(2,1)S(1)} %all-to-all-done.3.mine_ref), channel_id=1, source_target_pairs={{0,1},{1,0},{2,3},{3,2},{4,5},{5,4},{6,7},{7,6},{8,9},{9,8},{10,11... | collective-permute-start | bytes 1376264 | tf_op jit(solution)/shard_map/cond/branch_0_fun/ppermute | solution.py:709
  141.0 1.2 copy-start.4

commit v3 on v2

--- a/solution.py
+++ b/solution.py
@@ -746,11 +746,11 @@
 
     def first(faces):
         own, mask, low, high = prepare(place, counts, sends_x, features[0, 0], occupancy[0, 0], faces)
+        xl, xu = neighbours(low, high, ("xh", "y"), faces)
+        low, high = pick_y(place, sends_y, own, xl, xu, faces)
         later, low, high = lax.optimization_barrier((weight, low, high))
-        xl, xu = neighbours(low, high, ("xh", "y"), faces)
-        xl, xu, turned = lax.optimization_barrier((xl, xu, turn(later)))
-        low, high = pick_y(place, sends_y, own, xl, xu, faces)
         yl, yu = neighbours(low, high, ("xl", "z", "c"), faces)
+        yl, yu, turned = lax.optimization_barrier((yl, yu, turn(later)))
         table = (place, row_map, own, xl, xu, yl, yu, ahead, mask)
         conv_out, x9, stats = conv(*table) if faces else conv_steps(*table, True, False)
         return conv_out, x9, mask, turned, all_sum_parts(stats)

time: 143 us -> 143 us (level)
  transfers between devices with their start and end apart: 13 -> 13, of which waited for: 7 -> 8; matrix products, arithmetic and copies ran while one was open for 1% -> 1% of each run, Pallas kernels for 6% -> 6%
where the time goes in v3:
time: 143 us; the launch traced here: 142 us
  blocking collectives  48.5 us (34%)
  starting transfers between devices  39.9 us (28%)
  Pallas kernels  28.9 us (20%)
  waiting for transfers between devices  19.1 us (13%)
  local copies, waits for them, and re-layouts  2.75 us (2%)
  between operations  2.22 us (2%)
    all_to_all x1, blocking collectives, second(): parts = lax.all_to_all(join(keep, swap(send)), CROSS, 0, 0)  20.2 us
    ppermute x8, starting transfers between devices, neighbours(): return (lax.ppermute(first, axes, one), lax.ppermute(second, axes, two))  19.3 us
    all_to_all x1, blocking collectives, spread(): lax.all_to_all(jnp.broadcast_to(value[None], (size,) + value.shape), axes...  17.5 us
    all_to_all x2, starting transfers between devices, spread(): lax.all_to_all(jnp.broadcast_to(value[None], (size,) + value.shape), axes...  13.6 us
    all_to_all x1, blocking collectives, second(): parts = lax.all_to_all(middle(parts), 'z', 0, 0)  10.8 us
    all_to_all x2, waiting for transfers between devices, spread(): lax.all_to_all(jnp.broadcast_to(value[None], (size,) + value.shape), axes...  10.2 us
    pallas_call x1, Pallas kernels, wgrad(): pl.pallas_call(functools.partial(wgrad_kernel, unroll=unroll), out_shape=...  9.14 us
    pallas_call x1, Pallas kernels, conv_steps(): pl.pallas_call(functools.partial(step_kernel, forward=forward, faces=face...  6.01 us
  transfers between devices with their start and end apart: 13, of which 8 were waited for; matrix products, arithmetic and copies ran while one was open for 1% of the time, Pallas kernels for 6%

profile of v3, /device:TPU:1, one launch (start us, length us, event | category | flops | bytes accessed | tf_op | source)
XLA Modules:
  0.0 142.4 jit_solution(471892235554160487)
XLA Ops:
  1.4 0.1 pad_add_fusion.place_ref
  1.5 1.4 prepare.3
  2.9 0.7 collective-permute-start.16
  3.6 4.8 %collective-permute-start.17 = (bf16[2,64,128]{2,1,0:T(8,128)(2,1)S(1)}, bf16[2,64,128]{2,1,0:T(8,128)(2,1)S(1)}, u32[]{:S(2)}, u32[]{:S(2)}) collective-permute-start(bf16[2,64,128]{2,1,0:T(8,128)(2,1)S(1)} %get-tuple-element.156), channel_id=1, source_target_pairs={{0,32},{64,96},{128,160},{192,224},{32,0},{96,64},{160,128},{224,1... | collective-permute-start | bytes 98312 | tf_op jit(solution)/shard_map/ppermute | solution.py:188
  8.3 1.3 collective-permute-done.17.x2_ref.xu_ref
  9.6 0.9 pick_y.7
  10.5 5.2 %collective-permute-start.18 = (bf16[272,128]{1,0:T(8,128)(2,1)S(1)}, bf16[272,128]{1,0:T(8,128)(2,1)S(1)}, u32[]{:S(2)}, u32[]{:S(2)}) collective-permute-start(bf16[272,128]{1,0:T(8,128)(2,1)S(1)} %get-tuple-element.159), channel_id=1, source_target_pairs={{1,2},{3,4},{5,6},{7,8},{9,10},{11,12},{13,14},{15,16},{17,18},{19... | collective-permute-start | bytes 208904 | tf_op jit(solution)/shard_map/ppermute | solution.py:188
  15.8 0.1 collective-permute-start.19
  15.9 1.3 turn.3
  17.2 0.6 collective-permute-done.18.yl_ref
  17.8 0.0 copy-start.10
  17.8 0.0 copy-start.13
  17.8 0.0 copy-start.15
  17.8 5.7 %forward_conv.1 = (f32[4,512,128]{2,1,0:T(8,128)S(1)}, bf16[4,640,1152]{2,1,0:T(8,128)(2,1)}, f32[8,128]{1,0:T(8,128)S(1)}) custom-call(s32[3]{0:T(128)S(1)} %pad_add_fusion.place_ref, s32[4,27]{1,0:T(4,128)S(1)} %bitcast.40, s32[4,27]{1,0:T(4,128)S(1)} %bitcast.41, bf16[4,512,128]{2,1,0:T(8,128)(2,1)S(1)} %get-tuple-element.154.own_ref, ...), custom_call_target="tpu_custom_call" | custom-call | flops 6000000000 | bytes 12582912 | tf_op jit(solution)/shard_map/forward_conv/pallas_call | solution.py:322
  23.5 17.5 %all_to_all.57 = f32[16,8,128]{2,1,0:T(8,128)S(1)} all-to-all(f32[16,8,128]{2,1,0:T(8,128)S(1)} %broadcast_in_dim.20), channel_id=1, replica_groups=mesh['xh'=2,'y'=4,'xl'=2,'z'=8,'c'=2] {'z','c'}, dimensions={0} | all-to-all | bytes 131072 | tf_op jit(solution)/shard_map/all_to_all | solution.py:701
  41.1 0.6 broadcast_in_dim.21
  41.7 7.4 %all-to-all-start.11 = ((f32[16,8,128]{2,1,0:T(8,128)}), f32[16,8,128]{2,1,0:T(8,128)S(1)}, u32[]{:S(2)}, u32[]{:S(2)}) async-start(f32[16,8,128]{2,1,0:T(8,128)} %broadcast_in_dim.21), calls=%async_computation.11 | async-start | bytes 131072 | tf_op jit(solution)/shard_map/all_to_all | solution.py:701
  49.2 6.5 %all-to-all-done.11 = f32[16,8,128]{2,1,0:T(8,128)S(1)} async-done(((f32[16,8,128]{2,1,0:T(8,128)}), f32[16,8,128]{2,1,0:T(8,128)S(1)}, u32[]{:S(2)}, u32[]{:S(2)}) %all-to-all-start.11) | async-done | bytes 65568 | tf_op jit(solution)/shard_map/all_to_all | solution.py:701
  55.7 0.6 slice_reduce_fusion
  57.0 84.2 %conditional.1 = (bf16[4,512,128]{2,1,0:T(8,128)(2,1)}, bf16[4,512,128]{2,1,0:T(8,128)(2,1)}, f32[27,128,128]{2,1,0:T(8,128)S(1)}, f32[1,128]{1,0:T(1,128)}, f32[1,128]{1,0:T(1,128)}) conditional(s32[]{:T(128)} %convert_element_type.3, (bf16[1,1,4,512,128]{4,3,2,1,0:T(8,128)(2,1)}, s32[3]{0:T(128)S(1)}, f32[16,8,128]{2,1,0:T(8,128)S(1)}, ...), branch_computations={%region_2.3_spmd, %region_3.5_spmd} | conditional | flops 18012598272 | bytes 130105880 | solution.py:780
  57.0 0.0 copy-start.8
  57.0 9.1 %weight_terms.2 = (bf16[4,512,128]{2,1,0:T(8,128)(2,1)}, f32[4,512,128]{2,1,0:T(8,128)S(1)}, f32[8,128]{1,0:T(8,128)S(1)}, f32[3632,128]{1,0:T(8,128)S(1)}, bf16[3632,128]{1,0:T(8,128)(2,1)S(1)}) custom-call(s32[3]{0:T(128)S(1)} %get-tuple-element.48.place_ref, f32[16,8,128]{2,1,0:T(8,128)S(1)} %get-tuple-element.49.stat_ref, ...), custom_call_target="tpu_custom_call" | custom-call | flops 6000000000 | bytes 12582912 | tf_op jit(solution)/shard_map/cond/branch_0_fun/weight_terms/pallas_call | solution.py:532
  66.2 1.7 %collective-permute-start = (bf16[3632,128]{1,0:T(8,128)(2,1)S(1)}, bf16[3632,128]{1,0:T(8,128)(2,1)S(1)}, u32[]{:S(2)}, u32[]{:S(2)}) collective-permute-start(bf16[3632,128]{1,0:T(8,128)(2,1)S(1)} %get-tuple-element.58), channel_id=1, source_target_pairs={{0,1},{1,0},{2,3},{3,2},{4,5},{5,4},{6,7},{7,6},{8,9},{9,8},{10,11... | collective-permute-start | bytes 2789384 | tf_op jit(solution)/shard_map/cond/branch_0_fun/ppermute | solution.py:709
  67.9 2.1 %collective-permute-done.got_ref = bf16[3632,128]{1,0:T(8,128)(2,1)S(1)} collective-permute-done((bf16[3632,128]{1,0:T(8,128)(2,1)S(1)}, bf16[3632,128]{1,0:T(8,128)(2,1)S(1)}, u32[]{:S(2)}, u32[]{:S(2)}) %collective-permute-start) | collective-permute-done | bytes 929824 | tf_op jit(solution)/shard_map/cond/branch_0_fun/ppermute | solution.py:709
  70.0 0.2 join.2
  70.2 20.2 %all_to_all.50.parts_ref = bf16[16,272,128]{2,1,0:T(8,128)(2,1)S(1)} all-to-all(bf16[16,272,128]{2,1,0:T(8,128)(2,1)S(1)} %join.2), channel_id=1, replica_groups=mesh['xh'=2,'y'=4,'xl'=2,'z'=8,'c'=2] {'xh','y','xl'}, dimensions={0} | all-to-all | bytes 2228224 | tf_op jit(solution)/shard_map/cond/branch_0_fun/all_to_all | solution.py:762
  90.4 0.2 middle.2
  90.6 10.8 %all_to_all.51.parts_ref = f32[8,40,128]{2,1,0:T(8,128)S(1)} all-to-all(f32[8,40,128]{2,1,0:T(8,128)S(1)} %middle.2), channel_id=1, replica_groups=mesh['xh'=2,'y'=4,'xl'=2,'z'=8,'c'=2] {'z'}, dimensions={0} | all-to-all | bytes 327680 | tf_op jit(solution)/shard_map/cond/branch_0_fun/all_to_all | solution.py:763
  101.4 1.1 grad_conv.2
  102.5 0.0 copy-start.9
  102.5 1.3 combine.2
  103.8 3.3 %all-to-all-start.2 = ((bf16[8,16,128]{2,1,0:T(8,128)(2,1)}), bf16[8,16,128]{2,1,0:T(8,128)(2,1)S(1)}, u32[]{:S(2)}, u32[]{:S(2)}) async-start(bf16[8,16,128]{2,1,0:T(8,128)(2,1)} %get-tuple-element.65), calls=%async_computation.2 | async-start | bytes 65536 | tf_op jit(solution)/shard_map/cond/branch_0_fun/all_to_all | solution.py:768
  107.2 0.7 collective-permute-start.1
  107.8 2.0 %collective-permute-start.2 = (bf16[2,64,128]{2,1,0:T(8,128)(2,1)S(1)}, bf16[2,64,128]{2,1,0:T(8,128)(2,1)S(1)}, u32[]{:S(2)}, u32[]{:S(2)}) collective-permute-start(bf16[2,64,128]{2,1,0:T(8,128)(2,1)S(1)} %get-tuple-element.69), channel_id=1, source_target_pairs={{0,32},{64,96},{128,160},{192,224},{32,0},{96,64},{160,128},{224,1... | collective-permute-start | bytes 98312 | tf_op jit(solution)/shard_map/cond/branch_0_fun/ppermute | solution.py:188
  109.8 1.3 collective-permute-done.2.x2_ref.xu_ref
  111.1 0.8 pick_y.4
  111.9 2.1 %all-to-all-done.2 = bf16[8,16,128]{2,1,0:T(8,128)(2,1)S(1)} async-done(((bf16[8,16,128]{2,1,0:T(8,128)(2,1)}), bf16[8,16,128]{2,1,0:T(8,128)(2,1)S(1)}, u32[]{:S(2)}, u32[]{:S(2)}) %all-to-all-start.2) | async-done | bytes 32800 | tf_op jit(solution)/shard_map/cond/branch_0_fun/all_to_all | solution.py:768
  114.0 5.9 %collective-permute-start.3 = (bf16[272,128]{1,0:T(8,128)(2,1)S(1)}, bf16[272,128]{1,0:T(8,128)(2,1)S(1)}, u32[]{:S(2)}, u32[]{:S(2)}) collective-permute-start(bf16[272,128]{1,0:T(8,128)(2,1)S(1)} %get-tuple-element.74), channel_id=1, source_target_pairs={{1,2},{3,4},{5,6},{7,8},{9,10},{11,12},{13,14},{15,16},{17,18},{19... | collective-permute-start | bytes 208904 | tf_op jit(solution)/shard_map/cond/branch_0_fun/ppermute | solution.py:188
  119.8 0.1 collective-permute-start.4
  120.0 0.8 broadcast_in_dim.5
  120.8 6.2 %all-to-all-start.3 = ((bf16[16,112,128]{2,1,0:T(8,128)(2,1)}), bf16[16,112,128]{2,1,0:T(8,128)(2,1)S(1)}, u32[]{:S(2)}, u32[]{:S(2)}) async-start(bf16[16,112,128]{2,1,0:T(8,128)(2,1)} %broadcast_in_dim.5), calls=%async_computation.3 | async-start | bytes 917504 | tf_op jit(solution)/shard_map/cond/branch_0_fun/all_to_all | solution.py:701
  127.0 6.0 %transposed_conv.2 = bf16[4,512,128]{2,1,0:T(8,128)(2,1)} custom-call(s32[3]{0:T(128)S(1)} %get-tuple-element.48.place_ref, s32[4,27]{1,0:T(4,128)S(1)} %get-tuple-element.73.map_ref.rows_ref, s32[4,27]{1,0:T(4,128)S(1)} %get-tuple-element.73.map_ref.rows_ref, bf16[4,512,128]{2,1,0:T(8,128)(2,1)S(1)} %get-tuple-element.67.own_ref, ...), custom_call_target="tpu_custom_call" | custom-call | flops 6000000000 | bytes 12582912 | tf_op jit(solution)/shard_map/cond/branch_0_fun/transposed_conv/pallas_call | solution.py:393
  133.0 3.7 %all-to-all-done.3.mine_ref = bf16[16,112,128]{2,1,0:T(8,128)(2,1)S(1)} async-done(((bf16[16,112,128]{2,1,0:T(8,128)(2,1)}), bf16[16,112,128]{2,1,0:T(8,128)(2,1)S(1)}, u32[]{:S(2)}, u32[]{:S(2)}) %all-to-all-start.3) | async-done | bytes 458784 | tf_op jit(solution)/shard_map/cond/branch_0_fun/all_to_all | solution.py:701
  136.7 2.0 %collective-permute-start.5 = (bf16[16,112,128]{2,1,0:T(8,128)(2,1)S(1)}, bf16[16,112,128]{2,1,0:T(8,128)(2,1)S(1)}, u32[]{:S(2)}, u32[]{:S(2)}) collective-permute-start(bf16[16,112,128]{2,1,0:T(8,128)(2,1)S(1)} %all-to-all-done.3.mine_ref), channel_id=1, source_target_pairs={{0,1},{1,0},{2,3},{3,2},{4,5},{5,4},{6,7},{7,6},{8,9},{9,8},{10,11... | collective-permute-start | bytes 1376264 | tf_op jit(solution)/shard_map/cond/branch_0_fun/ppermute | solution.py:709
  138.7 1.4 %collective-permute-done.5.other_ref = bf16[16,112,128]{2,1,0:T(8,128)(2,1)S(1)} collective-permute-done((bf16[16,112,128]{2,1,0:T(8,128)(2,1)S(1)}, bf16[16,112,128]{2,1,0:T(8,128)(2,1)S(1)}, u32[]{:S(2)}, u32[]{:S(2)}) %collective-permute-start.5) | collective-permute-done | bytes 458784 | tf_op jit(solution)/shard_map/cond/branch_0_fun/ppermute | solution.py:709
  140.1 0.9 finish.2
  141.2 0.0 copy-start.4
  141.3 1.2 copy-done.4
  (29 shorter events, 0.1 us)
Async XLA Ops:
  0.6 15.2 %copy-start.2 = (bf16[27,128,128]{2,1,0:T(8,128)(2,1)S(1)}, bf16[27,128,128]{2,1,0:T(8,128)(2,1)}, u32[]{:S(2)}) copy-start(bf16[27,128,128]{2,1,0:T(8,128)(2,1)} %w_ref) | copy-start | bytes 2654212
  0.6 17.1 %copy-start.14 = (s32[1,1,4,27]{3,2,1,0:T(4,128)S(1)}, s32[1,1,4,27]{3,2,1,0:T(4,128)}, u32[]{:S(2)}) copy-start(s32[1,1,4,27]{3,2,1,0:T(4,128)} %param.15) | copy-start | bytes 1300
  2.9 5.4 %collective-permute-start.16 = (bf16[2,64,128]{2,1,0:T(8,128)(2,1)S(1)}, bf16[2,64,128]{2,1,0:T(8,128)(2,1)S(1)}, u32[]{:S(2)}, u32[]{:S(2)}) collective-permute-start(bf16[2,64,128]{2,1,0:T(8,128)(2,1)S(1)} %get-tuple-element.155), channel_id=1, source_target_pairs={{32,64},{96,128},{160,192},{64,32},{128,96},{192,160},{33,65},{97,... | collective-permute-start | bytes 98312 | tf_op jit(solution)/shard_map/ppermute | solution.py:188
  3.6 6.1 %collective-permute-start.17 = (bf16[2,64,128]{2,1,0:T(8,128)(2,1)S(1)}, bf16[2,64,128]{2,1,0:T(8,128)(2,1)S(1)}, u32[]{:S(2)}, u32[]{:S(2)}) collective-permute-start(bf16[2,64,128]{2,1,0:T(8,128)(2,1)S(1)} %get-tuple-element.156), channel_id=1, source_target_pairs={{0,32},{64,96},{128,160},{192,224},{32,0},{96,64},{160,128},{224,1... | collective-permute-start | bytes 98312 | tf_op jit(solution)/shard_map/ppermute | solution.py:188
  10.5 7.2 %collective-permute-start.18 = (bf16[272,128]{1,0:T(8,128)(2,1)S(1)}, bf16[272,128]{1,0:T(8,128)(2,1)S(1)}, u32[]{:S(2)}, u32[]{:S(2)}) collective-permute-start(bf16[272,128]{1,0:T(8,128)(2,1)S(1)} %get-tuple-element.159), channel_id=1, source_target_pairs={{1,2},{3,4},{5,6},{7,8},{9,10},{11,12},{13,14},{15,16},{17,18},{19... | collective-permute-start | bytes 208904 | tf_op jit(solution)/shard_map/ppermute | solution.py:188
  15.8 2.0 %collective-permute-start.19 = (bf16[272,128]{1,0:T(8,128)(2,1)S(1)}, bf16[272,128]{1,0:T(8,128)(2,1)S(1)}, u32[]{:S(2)}, u32[]{:S(2)}) collective-permute-start(bf16[272,128]{1,0:T(8,128)(2,1)S(1)} %get-tuple-element.160), channel_id=1, source_target_pairs={{0,1},{2,3},{4,5},{6,7},{8,9},{10,11},{12,13},{14,15},{16,17},{18,... | collective-permute-start | bytes 208904 | tf_op jit(solution)/shard_map/ppermute | solution.py:188
  17.8 39.2 %copy-start.3 = (bf16[1,1,4,512,128]{4,3,2,1,0:T(8,128)(2,1)S(1)}, bf16[1,1,4,512,128]{4,3,2,1,0:T(8,128)(2,1)}, u32[]{:S(2)}) copy-start(bf16[1,1,4,512,128]{4,3,2,1,0:T(8,128)(2,1)} %param.12) | copy-start | bytes 1572868
  17.8 39.2 %copy-start.10 = (s32[1,1,4,512]{3,2,1,0:T(4,128)S(1)}, s32[1,1,4,512]{3,2,1,0:T(4,128)}, u32[]{:S(2)}) copy-start(s32[1,1,4,512]{3,2,1,0:T(4,128)} %param.13) | copy-start | bytes 24580
  17.8 39.2 %copy-start.11 = (s32[1,1,2,2]{3,2,1,0:T(2,128)S(1)}, s32[1,1,2,2]{3,2,1,0:T(2,128)}, u32[]{:S(2)}) copy-start(s32[1,1,2,2]{3,2,1,0:T(2,128)} %param.16) | copy-start | bytes 52
  17.8 39.2 %copy-start.12 = (s32[1,1,2,4]{3,2,1,0:T(2,128)S(1)}, s32[1,1,2,4]{3,2,1,0:T(2,128)}, u32[]{:S(2)}) copy-start(s32[1,1,2,4]{3,2,1,0:T(2,128)} %param.17) | copy-start | bytes 100
  17.8 39.2 %copy-start.13 = (f32[128]{0:T(128)S(1)}, f32[128]{0:T(128)}, u32[]{:S(2)}) copy-start(f32[128]{0:T(128)} %param.19) | copy-start | bytes 1540
  17.8 39.2 %copy-start.15 = (f32[128]{0:T(128)S(1)}, f32[128]{0:T(128)}, u32[]{:S(2)}) copy-start(f32[128]{0:T(128)} %param.20) | copy-start | bytes 1540
  41.7 14.0 %all-to-all-start.11 = ((f32[16,8,128]{2,1,0:T(8,128)}), f32[16,8,128]{2,1,0:T(8,128)S(1)}, u32[]{:S(2)}, u32[]{:S(2)}) async-start(f32[16,8,128]{2,1,0:T(8,128)} %broadcast_in_dim.21), calls=%async_computation.11 | async-start | bytes 131072 | tf_op jit(solution)/shard_map/all_to_all | solution.py:701
  57.0 9.2 %copy-start.5 = (f32[4,512,128]{2,1,0:T(8,128)}, f32[4,512,128]{2,1,0:T(8,128)S(1)}, u32[]{:S(2)}) copy-start(f32[4,512,128]{2,1,0:T(8,128)S(1)} %get-tuple-element.50.conv_ref) | copy-start | bytes 3145732 | tf_op jit(solution)/shard_map/cond
  57.0 44.4 %copy-start.8 = (bf16[4,512,128]{2,1,0:T(8,128)(2,1)}, bf16[4,512,128]{2,1,0:T(8,128)(2,1)S(1)}, u32[]{:S(2)}) copy-start(bf16[4,512,128]{2,1,0:T(8,128)(2,1)S(1)} %get-tuple-element.52.mask_ref) | copy-start | bytes 1572868 | tf_op jit(solution)/shard_map/cond
  66.2 3.8 %collective-permute-start = (bf16[3632,128]{1,0:T(8,128)(2,1)S(1)}, bf16[3632,128]{1,0:T(8,128)(2,1)S(1)}, u32[]{:S(2)}, u32[]{:S(2)}) collective-permute-start(bf16[3632,128]{1,0:T(8,128)(2,1)S(1)} %get-tuple-element.58), channel_id=1, source_target_pairs={{0,1},{1,0},{2,3},{3,2},{4,5},{5,4},{6,7},{7,6},{8,9},{9,8},{10,11... | collective-permute-start | bytes 2789384 | tf_op jit(solution)/shard_map/cond/branch_0_fun/ppermute | solution.py:709
  70.2 31.2 %copy-start.6 = (f32[4,512,128]{2,1,0:T(8,128)S(1)}, f32[4,512,128]{2,1,0:T(8,128)}, u32[]{:S(2)}) copy-start(f32[4,512,128]{2,1,0:T(8,128)} %copy-done.5) | copy-start | bytes 3145732 | tf_op jit(solution)/shard_map/cond
  102.5 24.5 %copy-start.7 = (bf16[3,1152,128]{2,1,0:T(8,128)(2,1)S(1)}, bf16[3,1152,128]{2,1,0:T(8,128)(2,1)}, u32[]{:S(2)}) copy-start(bf16[3,1152,128]{2,1,0:T(8,128)(2,1)} %get-tuple-element.76.w_ref) | copy-start | bytes 2654212 | tf_op jit(solution)/shard_map/cond
  102.5 24.5 %copy-start.9 = (bf16[4,512,128]{2,1,0:T(8,128)(2,1)S(1)}, bf16[4,512,128]{2,1,0:T(8,128)(2,1)}, u32[]{:S(2)}) copy-start(bf16[4,512,128]{2,1,0:T(8,128)(2,1)} %copy-done.8) | copy-start | bytes 1572868 | tf_op jit(solution)/shard_map/cond
  103.8 10.1 %all-to-all-start.2 = ((bf16[8,16,128]{2,1,0:T(8,128)(2,1)}), bf16[8,16,128]{2,1,0:T(8,128)(2,1)S(1)}, u32[]{:S(2)}, u32[]{:S(2)}) async-start(bf16[8,16,128]{2,1,0:T(8,128)(2,1)} %get-tuple-element.65), calls=%async_computation.2 | async-start | bytes 65536 | tf_op jit(solution)/shard_map/cond/branch_0_fun/all_to_all | solution.py:768
  107.2 2.7 %collective-permute-start.1 = (bf16[2,64,128]{2,1,0:T(8,128)(2,1)S(1)}, bf16[2,64,128]{2,1,0:T(8,128)(2,1)S(1)}, u32[]{:S(2)}, u32[]{:S(2)}) collective-permute-start(bf16[2,64,128]{2,1,0:T(8,128)(2,1)S(1)} %get-tuple-element.68), channel_id=1, source_target_pairs={{32,64},{96,128},{160,192},{64,32},{128,96},{192,160},{33,65},{97,... | collective-permute-start | bytes 98312 | tf_op jit(solution)/shard_map/cond/branch_0_fun/ppermute | solution.py:188
  107.8 3.3 %collective-permute-start.2 = (bf16[2,64,128]{2,1,0:T(8,128)(2,1)S(1)}, bf16[2,64,128]{2,1,0:T(8,128)(2,1)S(1)}, u32[]{:S(2)}, u32[]{:S(2)}) collective-permute-start(bf16[2,64,128]{2,1,0:T(8,128)(2,1)S(1)} %get-tuple-element.69), channel_id=1, source_target_pairs={{0,32},{64,96},{128,160},{192,224},{32,0},{96,64},{160,128},{224,1... | collective-permute-start | bytes 98312 | tf_op jit(solution)/shard_map/cond/branch_0_fun/ppermute | solution.py:188
  114.0 13.0 %collective-permute-start.3 = (bf16[272,128]{1,0:T(8,128)(2,1)S(1)}, bf16[272,128]{1,0:T(8,128)(2,1)S(1)}, u32[]{:S(2)}, u32[]{:S(2)}) collective-permute-start(bf16[272,128]{1,0:T(8,128)(2,1)S(1)} %get-tuple-element.74), channel_id=1, source_target_pairs={{1,2},{3,4},{5,6},{7,8},{9,10},{11,12},{13,14},{15,16},{17,18},{19... | collective-permute-start | bytes 208904 | tf_op jit(solution)/shard_map/cond/branch_0_fun/ppermute | solution.py:188
  119.8 7.1 %collective-permute-start.4 = (bf16[272,128]{1,0:T(8,128)(2,1)S(1)}, bf16[272,128]{1,0:T(8,128)(2,1)S(1)}, u32[]{:S(2)}, u32[]{:S(2)}) collective-permute-start(bf16[272,128]{1,0:T(8,128)(2,1)S(1)} %get-tuple-element.75), channel_id=1, source_target_pairs={{0,1},{2,3},{4,5},{6,7},{8,9},{10,11},{12,13},{14,15},{16,17},{18,... | collective-permute-start | bytes 208904 | tf_op jit(solution)/shard_map/cond/branch_0_fun/ppermute | solution.py:188
  120.8 15.9 %all-to-all-start.3 = ((bf16[16,112,128]{2,1,0:T(8,128)(2,1)}), bf16[16,112,128]{2,1,0:T(8,128)(2,1)S(1)}, u32[]{:S(2)}, u32[]{:S(2)}) async-start(bf16[16,112,128]{2,1,0:T(8,128)(2,1)} %broadcast_in_dim.5), calls=%async_computation.3 | async-start | bytes 917504 | tf_op jit(solution)/shard_map/cond/branch_0_fun/all_to_all | solution.py:701
  136.7 3.4 %collective-permute-start.5 = (bf16[16,112,128]{2,1,0:T(8,128)(2,1)S(1)}, bf16[16,112,128]{2,1,0:T(8,128)(2,1)S(1)}, u32[]{:S(2)}, u32[]{:S(2)}) collective-permute-start(bf16[16,112,128]{2,1,0:T(8,128)(2,1)S(1)} %all-to-all-done.3.mine_ref), channel_id=1, source_target_pairs={{0,1},{1,0},{2,3},{3,2},{4,5},{5,4},{6,7},{7,6},{8,9},{9,8},{10,11... | collective-permute-start | bytes 1376264 | tf_op jit(solution)/shard_map/cond/branch_0_fun/ppermute | solution.py:709
  141.2 1.2 copy-start.4
